TPU v7x, 256 devices: a whole 4x4x8 slice. The times are simulated.
256 devices in a mesh: band: 2 (over z_hi), domain: 128 (over x, y, z_lo, core).
Axes of the slice: x: 4, y: 4, z: 8 (z_hi: 2, z_lo: 4; z = z_hi * 4 + z_lo), core: 2. Of those that a mesh axis runs over, the one named last changes fastest.
Arguments:
- orbitals: bfloat16 [1024, 128, 2048], P('band', 'domain')
- potential: float32 [128, 2048], P('domain'), may hold values from 0.25 to 6
Outputs:
- rotated: bfloat16 [1024, 128, 2048], P('band', 'domain')
- h_sub: float32 [1024, 1024], replicated
All inputs are finite; a program needn't handle non-finite values.
Results may differ from a plain program's by a relative error of at most 0.0058.
Values may be sent and summed in bfloat16 or wider, within the bound.
A program may use at most 128 MiB of HBM per device.

v0:
```python
import math

import jax
import jax.numpy as jnp
from jax import lax
from jax.sharding import PartitionSpec as P

BX = 4
BY = 4
NZ = 128
PY = 8


def shifted(block, axis, distance):
    devices = range(lax.axis_size(axis))
    route = [((i - distance) % len(devices), i) for i in devices]
    return lax.ppermute(block, axis, route)


def from_behind(block, axis, distance):
    devices = range(lax.axis_size(axis))
    route = [(i - distance, i) for i in devices if i - distance in devices]
    return lax.ppermute(block, axis, route)


def x_face(piece, offset):
    return shifted(piece, "domain", offset)


def y_face(piece, offset):
    return shifted(piece, "domain", offset)


def apply_padded(xpad, ypad, vgrid):
    xfield = xpad.astype(jnp.float32)
    yfield = ypad.astype(jnp.float32)
    center = xfield[:, 2:-2]
    xsum = (
        -30.0 * center
        + 16.0 * (xfield[:, 1:-3] + xfield[:, 3:-1])
        - (xfield[:, :-4] + xfield[:, 4:])
    )
    ysum = (
        -30.0 * center
        + 16.0 * (yfield[:, :, 1:-3] + yfield[:, :, 3:-1])
        - (yfield[:, :, :-4] + yfield[:, :, 4:])
    )
    zsum = -30.0 * center
    for step, weight in ((1, 16.0), (2, -1.0)):
        zsum = zsum + weight * (jnp.roll(center, step, axis=-1) + jnp.roll(center, -step, axis=-1))
    lap = (xsum + ysum + zsum) / 12.0
    return (-0.5 * lap + vgrid[None] * center).astype(jnp.bfloat16)


def mirror(matrix):
    return jnp.tril(matrix) + jnp.tril(matrix, -1).T


def shards(orbitals, potential):
    orb_g = orbitals.shape[0]
    cells = orbitals.shape[2]
    grid = orbitals.reshape(orb_g, BX, BY, NZ)
    vgrid = potential.reshape(BX, BY, NZ)
    column = lax.axis_index("domain") % PY
    from_below_x = x_face(grid[:, BX - 2 :], PY)
    from_above_x = x_face(grid[:, :2], -PY)
    top_rows = grid[:, :, BY - 2 :]
    bottom_rows = grid[:, :, :2]
    from_below_y = jnp.where(column == 0, y_face(top_rows, 1 - PY), y_face(top_rows, 1))
    from_above_y = jnp.where(column == PY - 1, y_face(bottom_rows, PY - 1), y_face(bottom_rows, -1))
    xpad = jnp.concatenate([from_below_x, grid, from_above_x], axis=1)
    ypad = jnp.concatenate([from_below_y, grid, from_above_y], axis=2)
    group = math.gcd(orb_g, 16)
    xblocks = xpad.reshape((orb_g // group, group) + xpad.shape[1:])
    yblocks = ypad.reshape((orb_g // group, group) + ypad.shape[1:])
    hpsi = lax.map(lambda pair: apply_padded(pair[0], pair[1], vgrid), (xblocks, yblocks))
    flat = orbitals.reshape(orb_g, cells)
    hflat = hpsi.reshape(orb_g, cells)
    band_id = lax.axis_index("band")
    first_group = band_id == 0
    received = from_behind(flat, "band", 1)
    upper_part = jnp.where(first_group, flat, received)
    lower_part = jnp.where(first_group, jnp.zeros_like(flat), flat)
    stacked = jnp.concatenate([upper_part, lower_part], axis=0)
    s_rows = jnp.dot(flat, stacked.T, preferred_element_type=jnp.float32)
    h_rows = jnp.dot(hflat, stacked.T, preferred_element_type=jnp.float32)
    local_sum = jnp.sum(potential)
    total_orb = stacked.shape[0]
    pot_total = lax.psum(local_sum, "domain")
    s_summed, h_summed = lax.psum((s_rows, h_rows), "domain")
    s_full, h_full = (
        lax.all_gather(s_summed, "band", axis=0, tiled=True),
        lax.all_gather(h_summed, "band", axis=0, tiled=True),
    )
    intersection = mirror(s_full)
    ham_hat = mirror(h_full)
    vmean = pot_total / (lax.axis_size("domain") * cells)
    ham = ham_hat - vmean * intersection
    chol = jnp.linalg.cholesky(intersection)
    linv = lax.linalg.triangular_solve(
        chol, jnp.eye(total_orb, dtype=jnp.float32), left_side=True, lower=True
    )
    h_sub = jnp.dot(
        jnp.dot(linv, ham, precision=lax.Precision.HIGHEST), linv.T, precision=lax.Precision.HIGHEST
    )
    rot_rows = lax.dynamic_slice_in_dim(linv, band_id * orb_g, orb_g, 0).astype(jnp.bfloat16)
    rotated = jnp.dot(rot_rows, stacked, preferred_element_type=jnp.float32).astype(jnp.bfloat16)
    return (rotated.reshape(orbitals.shape), h_sub)


def solution(mesh):
    in_specs = (P("band", "domain", None), P("domain", None))
    out_specs = (P("band", "domain", None), P())
    return jax.shard_map(shards, mesh=mesh, in_specs=in_specs, out_specs=out_specs, check_vma=False)
```

profile of v0, /device:TPU:1, one launch (start us, length us, event | category | flops | bytes accessed | tf_op | source)
XLA Modules:
  0.0 2311.3 jit_solution(14866953766530692514)
XLA Ops:
  7.2 3.2 reshape.100
  10.4 2.5 fusion.108
  12.9 7.7 collective-permute-start.3
  23.2 20.1 collective-permute-done.3
  43.3 3.2 concatenate.71
  46.5 19.2 collective-permute-done.4
  65.7 9.7 collective-permute-start
  78.1 4.9 pad_maximum_fusion.2
  83.2 5.7 pad_maximum_fusion.1
  88.9 112.9 %while.13 = (s32[]{:T(128)}, bf16[32,16,4,4,128]{4,3,2,1,0:T(4,128)(2,1)}, bf16[32,16,8,4,128]{4,3,2,1,0:T(4,128)(2,1)}, bf16[32,16,4,8,128]{4,3,2,1,0:T(8,128)(2,1)}, f32[1,2048]{1,0:T(1,128)S(1)}, /*index=5*/s32[]{:T(128)}) while((s32[]{:T(128)}, bf16[32,16,4,4,128]{4,3,2,1,0:T(4,128)(2,1)}, bf16[32,16,8,4,128]{4,3,2,1,0:T(4,128)(2,1)}, ...), condition=%wide.region_18.19_spmd, body=%wide.region_17.18_spmd.sunk | while | flops 1015810 | bytes 3613261 | solution.py:76
  201.9 4.6 reshape.101
  206.8 3.7 convolution_bitcast_fusion
  210.6 3.7 fusion.47
  214.4 1311.9 %all-reduce.4.cloned.1.call-done = (f32[512,1024]{1,0:T(8,128)}, f32[512,1024]{1,0:T(8,128)}) async-done(((f32[512,1024]{1,0:T(8,128)}, f32[512,1024]{1,0:T(8,128)}), (f32[512,1024]{1,0:T(8,128)}, f32[512,1024]{1,0:T(8,128)})) %all-reduce.4.cloned.1.call-update) | async-done | bytes 4194320 | tf_op jit(solution)/shard_map/psum | solution.py:90
  1526.9 353.7 %psum.23 = f32[]{:T(128)} all-reduce(f32[]{:T(128)} %reduce_sum.9), channel_id=1, replica_groups=mesh['band'=2,'domain'=128] {'domain'}, use_global_device_ids=true, to_apply=%region_21.22 | all-reduce | flops 1 | bytes 8 | tf_op jit(solution)/shard_map/psum | solution.py:89
  1881.7 2.5 fusion.48
  1884.2 4.8 fusion.22
  1889.0 5.4 copy.5
  1894.3 7.0 bitcast_add_fusion.2
  1901.4 5.6 copy.6
  1906.9 4.4 fusion.18
  1913.4 11.7 cholesky.222
  1925.1 2.5 cholesky.254
  1927.6 9.8 custom-call.62
  1941.4 11.9 cholesky.243
  1953.9 9.8 custom-call.63
  1967.1 11.7 cholesky.466
  1980.1 9.8 custom-call.64
  1993.5 12.1 cholesky.485
  2006.8 9.8 custom-call.65
  2020.1 11.7 cholesky.504
  2033.2 9.9 custom-call.66
  2046.4 11.7 cholesky.524
  2059.5 9.8 custom-call.67
  2072.3 11.9 cholesky.544
  2085.4 9.8 custom-call.68
  2097.9 11.7 cholesky.562
  2116.3 4.8 select_select_fusion
  2121.2 23.6 %while.14 = (s32[]{:T(128)}, f32[1024,1024]{1,0:T(8,128)}, s32[8,2]{0,1:T(2,128)S(1)}, f32[8,128,128]{2,1,0:T(8,128)S(1)}, s32[]{:T(128)}) while((s32[]{:T(128)}, f32[1024,1024]{1,0:T(8,128)}, s32[8,2]{0,1:T(2,128)S(1)}, f32[8,128,128]{2,1,0:T(8,128)S(1)}, s32[]{:T(128)}) %tuple.100), condition=%wide.while_cond, body=%wide.while_body.sunk | while | flops 2 | bytes 131181 | solution.py:100
  2144.8 79.0 %custom-call.69 = f32[8,128,128]{1,2,0:T(8,128)S(1)} custom-call(f32[8,128,128]{2,1,0:T(8,128)S(1)} %get-tuple-element.75), custom_call_target="InvertDiagBlocksLowerTriangular" | custom-call | tf_op jit(solution)/shard_map/triangular_solve | solution.py:100
  2239.0 2.6 convolution_subtract_fusion.2
  2243.1 2.8 convolution_subtract_fusion.1
  2247.4 3.4 convolution_subtract_fusion.3
  2250.8 4.7 fusion.21
  2255.6 5.3 copy.7
  2262.3 20.3 fusion.16
  2282.6 16.7 fusion.110
  2299.3 5.2 fusion.23
  (343 shorter events, 195.7 us)
Async XLA Ops:
  7.2 1519.1 %all-reduce.4.cloned.1.call-start = ((), (), s32[]{:S(2)}) async-start(), calls=%async_computation.2 | async-start | bytes 8388608 | tf_op jit(solution)/shard_map/psum | solution.py:90
  12.9 30.3 %collective-permute-start.3 = (bf16[512,4,2,128]{3,2,1,0:T(2,128)(2,1)}, bf16[512,4,2,128]{3,2,1,0:T(2,128)(2,1)}, u32[]{:S(2)}, u32[]{:S(2)}) collective-permute-start(bf16[512,4,2,128]{3,2,1,0:T(2,128)(2,1)} %get-tuple-element.106), channel_id=1, source_target_pairs={{7,0},{8,1},{9,2},{10,3},{11,4},{12,5},{13,6},{14,7},{15,8},{16,9}... | collective-permute-start | bytes 3145736 | tf_op jit(solution)/shard_map/ppermute | solution.py:17
  20.6 45.1 %collective-permute-start.4 = (bf16[512,4,2,128]{3,2,1,0:T(2,128)(2,1)}, bf16[512,4,2,128]{3,2,1,0:T(2,128)(2,1)}, u32[]{:S(2)}, u32[]{:S(2)}) collective-permute-start(bf16[512,4,2,128]{3,2,1,0:T(2,128)(2,1)} %get-tuple-element.106), channel_id=1, source_target_pairs={{127,0},{0,1},{1,2},{2,3},{3,4},{4,5},{5,6},{6,7},{7,8},{8,9},{9,1... | collective-permute-start | bytes 3145736 | tf_op jit(solution)/shard_map/ppermute | solution.py:17
  20.6 56.2 %collective-permute-start.5 = (bf16[512,4,2,128]{3,2,1,0:T(2,128)(2,1)}, bf16[512,4,2,128]{3,2,1,0:T(2,128)(2,1)S(1)}, u32[]{:S(2)}, u32[]{:S(2)}) collective-permute-start(bf16[512,4,2,128]{3,2,1,0:T(2,128)(2,1)} %get-tuple-element.107), channel_id=1, source_target_pairs={{121,0},{122,1},{123,2},{124,3},{125,4},{126,5},{127,6},{0,7},{1,8... | collective-permute-start | bytes 3145736 | tf_op jit(solution)/shard_map/ppermute | solution.py:17
  20.6 56.2 %collective-permute-start.6 = (bf16[512,4,2,128]{3,2,1,0:T(2,128)(2,1)}, bf16[512,4,2,128]{3,2,1,0:T(2,128)(2,1)}, u32[]{:S(2)}, u32[]{:S(2)}) collective-permute-start(bf16[512,4,2,128]{3,2,1,0:T(2,128)(2,1)} %get-tuple-element.107), channel_id=1, source_target_pairs={{1,0},{2,1},{3,2},{4,3},{5,4},{6,5},{7,6},{8,7},{9,8},{10,9},{11,1... | collective-permute-start | bytes 3145736 | tf_op jit(solution)/shard_map/ppermute | solution.py:17
  23.2 60.0 %collective-permute-start.1 = (bf16[512,2,4,128]{3,2,1,0:T(4,128)(2,1)}, bf16[512,2,4,128]{3,2,1,0:T(4,128)(2,1)}, u32[]{:S(2)}, u32[]{:S(2)}) collective-permute-start(bf16[512,2,4,128]{3,2,1,0:T(4,128)(2,1)} %get-tuple-element.108), channel_id=1, source_target_pairs={{120,0},{121,1},{122,2},{123,3},{124,4},{125,5},{126,6},{127,7},{0... | collective-permute-start | bytes 3145736 | tf_op jit(solution)/shard_map/ppermute | solution.py:17
  43.3 40.0 %collective-permute-start.2 = (bf16[512,2,4,128]{3,2,1,0:T(4,128)(2,1)}, bf16[512,2,4,128]{3,2,1,0:T(4,128)(2,1)}, u32[]{:S(2)}, u32[]{:S(2)}) collective-permute-start(bf16[512,2,4,128]{3,2,1,0:T(4,128)(2,1)} %get-tuple-element.109), channel_id=1, source_target_pairs={{8,0},{9,1},{10,2},{11,3},{12,4},{13,5},{14,6},{15,7},{16,8},{17,9... | collective-permute-start | bytes 3145736 | tf_op jit(solution)/shard_map/ppermute | solution.py:17
  65.7 140.8 %collective-permute-start = (bf16[512,2048]{1,0:T(8,128)(2,1)}, bf16[512,2048]{1,0:T(8,128)(2,1)}, u32[]{:S(2)}, u32[]{:S(2)}) collective-permute-start(bf16[512,2048]{1,0:T(8,128)(2,1)} %bitcast.152), channel_id=1, source_target_pairs={{0,128},{1,129},{2,130},{3,131},{4,132},{5,133},{6,134},{7,135},{8... | collective-permute-start | bytes 6291464 | tf_op jit(solution)/shard_map/ppermute | solution.py:23
  83.2 5.7 copy-start.8
  201.9 4.6 copy-start
  206.8 3.8 copy-start.4
  206.8 3.8 copy-start.6
  206.8 3.8 copy-start.3
  214.3 1669.9 %all-gather.3.cloned.1.call-start = ((), (), s32[]{:S(2)}) async-start(), calls=%async_computation | async-start | bytes 6291456 | tf_op jit(solution)/shard_map/all_gather | solution.py:92
  1526.3 724.5 %all-gather.5.cloned.1.call-start = ((), (), s32[]{:S(2)}) async-start(), calls=%async_computation.1 | async-start | bytes 6291456 | tf_op jit(solution)/shard_map/all_gather | solution.py:93
  1911.4 2.0 copy-start.2
  2223.8 4.7 copy-start.1
  2282.6 16.7 copy-start.5
  2282.6 16.7 copy-start.7
Sparse Core Ops, SparseCore 0:
  214.4 1311.7 all-reduce.3
  1528.2 112.9 all-gather.2
  1884.3 111.0 all-gather.4
where the time goes:
time: 2320 us; the launch traced here: 2310 us
  waiting for transfers between devices  1350 us (58%)
  other arithmetic  389 us (17%)
  blocking collectives  354 us (15%)
  matrix products  101 us (4%)
  local copies, waits for them, and re-layouts  76.8 us (3%)
    psum x1, waiting for transfers between devices, shards(): s_summed, h_summed = lax.psum((s_rows, h_rows), 'domain')  1310 us
    psum x1, blocking collectives, shards(): pot_total = lax.psum(local_sum, 'domain')  354 us
    another operation x30, other arithmetic, shards(): chol = jnp.linalg.cholesky(intersection)  172 us
    another operation x3, other arithmetic, shards(): lax.linalg.triangular_solve(chol, jnp.eye(total_orb, dtype=jnp.float32),...  83.8 us
  transfers between devices with their start and end apart: 10, of which 4 were waited for; matrix products, arithmetic and copies ran while one was open for 22% of the time, Pallas kernels for 0%

commit v1 on v0

v1 whole, which is shorter than its diff:
```python
import functools

import jax
import jax.numpy as jnp
from jax import lax
from jax.experimental import pallas as pl
from jax.experimental.pallas import tpu as pltpu
from jax.sharding import PartitionSpec as P

MESH = pl.DeviceIdType.MESH
HI = lax.Precision.HIGHEST
NN = (((1,), (0,)), ((), ()))
NT = (((1,), (1,)), ((), ()))
TN = (((0,), (0,)), ((), ()))
F32 = jnp.float32
BF16 = jnp.bfloat16
VMEM = pl.BlockSpec(memory_space=pltpu.VMEM)
MIB = 2**20
CELLS = 2048
HALF = 512
TILES_UP = ((0, 0), (0, 1), (1, 1))
TILES_LOW = ((0, 0), (1, 0), (1, 1))
TILES_ALL = ((0, 0), (0, 1), (1, 0), (1, 1))


def fdot(a, b, dims=NN):
    return lax.dot_general(a, b, dims, precision=HI, preferred_element_type=F32)


def bdot(a, b, dims=NN):
    return lax.dot_general(a, b, dims, preferred_element_type=F32)


def call(kernel, outs, args, name, scratch=(), collective=None, limit=48, flops=0):
    params = dict(vmem_limit_bytes=limit * MIB)
    if collective is not None:
        params.update(collective_id=collective, has_side_effects=True)
    return pl.pallas_call(
        kernel,
        out_shape=outs,
        in_specs=[VMEM] * len(args),
        out_specs=jax.tree.map(lambda _: VMEM, outs),
        scratch_shapes=list(scratch),
        compiler_params=pltpu.CompilerParams(**params),
        cost_estimate=pl.CostEstimate(flops=flops, bytes_accessed=8 * MIB, transcendentals=0),
        name=name,
    )(*args)


def own_overlap_kernel(orb, pot, pay):
    for t, (r, c) in enumerate(TILES_UP):
        tile = bdot(orb[256 * r : 256 * r + 256, :], orb[256 * c : 256 * c + 256, :], NT)
        pay[2 * t] = tile[:, :128]
        pay[2 * t + 1] = tile[:, 128:]
    pay[0, 128:136, :] = pot[0:8, :] + pot[8:16, :]


def all_sum_kernel(n_both, n_one, *refs):
    refs = list(refs)
    sizes = [(n, mode) for n, mode in ((n_both, "both"), (n_one, "one")) if n]
    n = len(sizes)
    pays, outs, rest = refs[:n], refs[n : 2 * n], refs[2 * n :]
    bufs = [rest[4 * i : 4 * i + 4] for i in range(n)]
    sems = rest[4 * n :]
    s1, r1, s2, r2, s3, r3, s4, r4, s5, r5 = sems
    band = lax.axis_index("band")
    dom = lax.axis_index("domain")
    x, y = dom // 32, (dom // 8) % 4
    z, core = (dom // 2) % 4, dom % 2
    here = x * 4 + y
    zz = band * 4 + z

    def at(b, xx, yy, zl, cc):
        return (b, ((xx * 4 + yy) * 4 + zl) * 2 + cc)

    partner = at(band, x, y, z, 1 - core)

    def xy_peer(k):
        xx, yy = (x + k // 4) % 4, (y + k % 4) % 4
        return at(band, xx, yy, z, core), xx * 4 + yy

    def xy_source(k):
        return ((x + 4 - k // 4) % 4) * 4 + (y + 4 - k % 4) % 4

    def z_peer(k):
        other = (zz + k) % 8
        return at(other // 4, x, y, other % 4, core)

    barrier = pltpu.get_barrier_semaphore()
    pl.semaphore_signal(barrier, inc=1, device_id=partner, device_id_type=MESH)
    for k in range(1, 16):
        pl.semaphore_signal(barrier, inc=1, device_id=xy_peer(k)[0], device_id_type=MESH)
    for k in range(1, 8):
        pl.semaphore_signal(barrier, inc=1, device_id=z_peer(k), device_id_type=MESH)
    pl.semaphore_wait(barrier, 23)

    def when(mode, body, condition=None):
        if mode == "one":
            pl.when(band == 1 if condition is None else condition)(body)
        else:
            body()

    def remote(src, dst, send, recv, device):
        return pltpu.make_async_remote_copy(
            src_ref=src, dst_ref=dst, send_sem=send, recv_sem=recv, device_id=device, device_id_type=MESH
        )

    mine = pl.ds(pl.multiple_of(core * 128, 128), 128)
    theirs = pl.ds(pl.multiple_of((1 - core) * 128, 128), 128)

    firsts = []
    for i, (_, mode) in enumerate(sizes):
        copy = remote(pays[i].at[:, theirs, :], bufs[i][0], s1.at[i], r1.at[i], partner)
        when(mode, copy.start)
        firsts.append(copy)
    seconds = []
    for i, (_, mode) in enumerate(sizes):
        pay, (half, whole, got, _) = pays[i], bufs[i]

        def second(i=i, pay=pay, half=half, whole=whole, got=got):
            firsts[i].wait()
            whole[...] = pay[:, mine, :] + half[...]
            for k in range(1, 16):
                device, there = xy_peer(k)
                rows = pl.ds(pl.multiple_of(there * 8, 8), 8)
                remote(whole.at[:, rows, :], got.at[k], s2.at[i, k], r2.at[i, k], device).start()

        when(mode, second)
    for i, (_, mode) in enumerate(sizes):
        whole, got, along = bufs[i][1:]

        def third(i=i, whole=whole, got=got, along=along):
            rows = pl.ds(pl.multiple_of(here * 8, 8), 8)
            for k in range(1, 16):
                remote(whole.at[:, rows, :], got.at[k], s2.at[i, k], r2.at[i, k], xy_peer(k)[0]).wait()
            total = whole[:, rows, :]
            for k in range(1, 16):
                total = total + got[k]
            along[zz] = total
            for k in range(1, 8):
                remote(along.at[zz], along.at[zz], s3.at[i, k], r3.at[i, k], z_peer(k)).start()

        when(mode, third)
    place = pl.ds(pl.multiple_of(core * 128 + here * 8, 8), 8)

    def spot(out, mode, rows):
        return out.at[:, :, rows, :] if mode == "both" else out.at[:, rows, :]

    for i, (_, mode) in enumerate(sizes):
        along, out = bufs[i][3], outs[i]
        for k in range(1, 8):
            source = (zz + 8 - k) % 8
            copy = remote(along.at[zz], along.at[source], s3.at[i, k], r3.at[i, k], z_peer(k))
            when(mode, copy.wait_send)
            when(mode, copy.wait_recv, source >= 4)
        upper = along[4] + along[5] + along[6] + along[7]
        if mode == "both":
            out[0, :, place, :] = along[0] + along[1] + along[2] + along[3]
            out[1, :, place, :] = upper
        else:
            out[:, place, :] = upper
        for k in range(1, 16):
            here_spot = spot(out, mode, place)
            remote(here_spot, here_spot, s4.at[i, k], r4.at[i, k], xy_peer(k)[0]).start()
        here_spot = spot(out, mode, place)
        remote(here_spot, here_spot, s5.at[i, 0], r5.at[i, 0], partner).start()
    for i, (_, mode) in enumerate(sizes):
        out = outs[i]
        for k in range(1, 16):
            rows = pl.ds(pl.multiple_of(core * 128 + xy_source(k) * 8, 8), 8)
            there = spot(out, mode, rows)
            remote(there, there, s4.at[i, k], r4.at[i, k], xy_peer(k)[0]).wait_recv()
            remote(there, there, s5.at[i, k], r5.at[i, k], partner).start()
    for i, (_, mode) in enumerate(sizes):
        out = outs[i]
        here_spot = spot(out, mode, place)
        for k in range(1, 16):
            remote(here_spot, here_spot, s4.at[i, k], r4.at[i, k], xy_peer(k)[0]).wait_send()
        for k in range(16):
            remote(here_spot, here_spot, s5.at[i, k], r5.at[i, k], partner).wait()


def all_sum(both, one, collective, name):
    args, outs, scratch = [], [], []
    if both is not None:
        args.append(both)
        outs.append(jax.ShapeDtypeStruct((2,) + both.shape, F32))
    if one is not None:
        args.append(one)
        outs.append(jax.ShapeDtypeStruct(one.shape, F32))
    for array in args:
        n = array.shape[0]
        scratch += [
            pltpu.VMEM((n, 128, 128), F32),
            pltpu.VMEM((n, 128, 128), F32),
            pltpu.VMEM((16, n, 8, 128), F32),
            pltpu.VMEM((8, n, 8, 128), F32),
        ]
    n = len(args)
    dma = pltpu.SemaphoreType.DMA
    scratch += [dma((n,)), dma((n,)), dma((n, 16)), dma((n, 16)), dma((n, 8)), dma((n, 8))]
    scratch += [dma((n, 16)), dma((n, 16)), dma((n, 16)), dma((n, 16))]
    n_both = 0 if both is None else both.shape[0]
    n_one = 0 if one is None else one.shape[0]
    return call(
        functools.partial(all_sum_kernel, n_both, n_one),
        outs,
        args,
        name,
        scratch=scratch,
        collective=collective,
        flops=10**9,
    )


def invert_block(block):
    lane = lax.broadcasted_iota(jnp.int32, (8, 128), 1)
    sub = lax.broadcasted_iota(jnp.int32, (8, 128), 0)
    rows = [block[8 * p : 8 * p + 8] for p in range(16)]
    for p in range(16):
        k = 8 * p
        panel = rows[p]
        d = [[jnp.broadcast_to(panel[i : i + 1, k + j : k + j + 1], (8, 128)) for j in range(i + 1)] for i in range(8)]
        inside = (lane >= k) & (lane < k + 8)
        start = jnp.where(inside, (lane == k + sub).astype(F32), panel)
        acc = [jnp.broadcast_to(start[s : s + 1, :], (8, 128)) for s in range(8)]
        done = []
        for j in range(8):
            r = lax.rsqrt(d[j][j])
            xj = acc[j] * r
            done.append(xj)
            low = [None] * 8
            for i in range(j + 1, 8):
                low[i] = d[i][j] * r
            for i in range(j + 1, 8):
                for m in range(j + 1, i + 1):
                    d[i][m] = d[i][m] - low[i] * low[m]
                acc[i] = acc[i] - low[i] * xj
        x = done[0]
        for s in range(1, 8):
            x = jnp.where(sub == s, done[s], x)
        rows[p] = x
        if p < 15:
            right = jnp.where(lane >= k + 8, x, 0.0)
            update = fdot(right, x, TN)
            for q in range(p + 1, 16):
                rows[q] = jnp.where(inside, 0.0, rows[q]) - update[8 * q : 8 * q + 8]
    whole = jnp.concatenate(rows, axis=0)
    rr = lax.broadcasted_iota(jnp.int32, (128, 128), 0)
    cc = lax.broadcasted_iota(jnp.int32, (128, 128), 1)
    return jnp.where(cc <= rr, whole, 0.0)


def eliminate(c, offset):
    blocks = c.shape[0] // 128
    rr = lax.broadcasted_iota(jnp.int32, (128, 128), 0)
    cc = lax.broadcasted_iota(jnp.int32, (128, 128), 1)

    @pl.loop(0, blocks)
    def _(j):
        rows = pl.ds(pl.multiple_of(j * 128, 128), 128)
        cols = pl.ds(pl.multiple_of(offset + j * 128, 128), 128)
        inverse = invert_block(c[rows, cols])
        c[rows, cols] = (rr == cc).astype(F32)
        c[rows, :] = fdot(inverse, c[rows, :])

        @pl.loop(j + 1, blocks)
        def _(i):
            below = pl.ds(pl.multiple_of(i * 128, 128), 128)
            across = pl.ds(pl.multiple_of(offset + i * 128, 128), 128)
            factor = c[rows, across]
            c[below, cols] = jnp.zeros((128, 128), F32)
            c[below, :] = c[below, :] - fdot(factor, c[rows, :], TN)

    for i in range(blocks):
        for j in range(i + 1, blocks):
            c[128 * i : 128 * i + 128, offset + 128 * j : offset + 128 * j + 128] = jnp.zeros((128, 128), F32)


def spread(c, slabs, tiles, offset):
    for t, (r, col) in enumerate(tiles):
        for h in range(2):
            lo = offset + 256 * col + 128 * h
            c[256 * r : 256 * r + 256, lo : lo + 128] = slabs(2 * t + h)


def first_factor_kernel(s, w):
    w[256:512, 0:256] = jnp.zeros((256, 256), F32)
    spread(w, lambda i: s[0, i], TILES_UP, 0)
    eliminate(w, 0)


def split(a):
    high = a.astype(BF16)
    return high, (a - high.astype(F32)).astype(BF16)


def dot3(a, b, dims=NN):
    return bdot(a[0], b[0], dims) + (bdot(a[0], b[1], dims) + bdot(a[1], b[0], dims))


def last_kernel(s, hown, cross, w0, h_sub, rot_other, rot_own, c, cross_s, wh, wl, mh, ml):
    band = lax.axis_index("band")
    for t, (r, col) in enumerate(TILES_ALL):
        for h in range(2):
            lo = 256 * col + 128 * h
            cross_s[256 * r : 256 * r + 256, lo : lo + 128] = cross[2 * t + h]
    low = fdot(cross_s[...], w0[...], NT)
    c[256:512, 512:768] = jnp.zeros((256, 256), F32)
    spread(c, lambda i: s[1, i], TILES_UP, 512)
    c[:, 512:1024] = c[:, 512:1024] - fdot(low, low, NT)
    c[:, 0:512] = -fdot(low, w0[...])
    eliminate(c, 512)

    @pl.when(band == 0)
    def _():
        rot_own[...] = w0[...].astype(BF16)
        rot_other[...] = jnp.zeros((512, 512), BF16)

    @pl.when(band == 1)
    def _():
        rot_own[...] = c[:, 512:1024].astype(BF16)
        rot_other[...] = c[:, 0:512].astype(BF16)

    for r in range(4):
        source = w0 if r < 2 else c
        base = 256 * (r % 2)
        width = 512 if r < 2 else 1024
        high, lowpart = split(source[base : base + 256, :])
        wh[256 * r : 256 * r + 256, 0:width] = high
        wl[256 * r : 256 * r + 256, 0:width] = lowpart

    rr = lax.broadcasted_iota(jnp.int32, (256, 256), 0)
    cc = lax.broadcasted_iota(jnp.int32, (256, 256), 1)
    weight = jnp.where(cc < rr, 1.0, jnp.where(cc == rr, 0.5, 0.0)).astype(F32)

    def pair(slabs, t):
        return jnp.concatenate([slabs(2 * t), slabs(2 * t + 1)], axis=1)

    half = {}
    for b in range(2):
        for t, (r, col) in enumerate(TILES_LOW):
            tile = pair(lambda i: hown[b, i], t)
            if r == col:
                tile = tile * weight
            half[2 * b + r, 2 * b + col] = split(tile)
    for t, (r, col) in enumerate(TILES_ALL):
        half[2 + r, col] = split(pair(lambda i: cross[8 + i], t))

    def block(high, lowpart, r, col):
        rows, cols = slice(256 * r, 256 * r + 256), slice(256 * col, 256 * col + 256)
        return high[rows, cols], lowpart[rows, cols]

    for r in range(4):
        for col in range(r + 1):
            total = None
            for k in range(col, r + 1):
                part = dot3(block(wh, wl, r, k), half[k, col])
                total = part if total is None else total + part
            high, lowpart = split(total)
            mh[256 * r : 256 * r + 256, 256 * col : 256 * col + 256] = high
            ml[256 * r : 256 * r + 256, 256 * col : 256 * col + 256] = lowpart

    vmean = jnp.sum(s[0, 0, 128:136, :]) / (128 * CELLS)
    shift = jnp.where(rr == cc, vmean, 0.0)

    def product(r, col):
        total = None
        for k in range(min(r, col) + 1):
            part = dot3(block(mh, ml, r, k), block(wh, wl, col, k), NT)
            total = part if total is None else total + part
        return total

    for r in range(4):
        for col in range(r + 1):
            tile = product(r, col)
            if r == col:
                h_sub[256 * r : 256 * r + 256, 256 * r : 256 * r + 256] = tile + tile.T - shift
            else:
                tile = tile + product(col, r).T
                h_sub[256 * r : 256 * r + 256, 256 * col : 256 * col + 256] = tile
                h_sub[256 * col : 256 * col + 256, 256 * r : 256 * r + 256] = tile.T


def ham_kernel(orb, xlo, xhi, ylo, yhi, pot, hpsi, pay):
    row = lax.broadcasted_iota(jnp.int32, (128, 128), 0)
    col = lax.broadcasted_iota(jnp.int32, (128, 128), 1)
    away = (row - col + 128) % 128
    circle = jnp.where(
        away == 0,
        -90.0,
        jnp.where((away == 1) | (away == 127), 16.0, jnp.where((away == 2) | (away == 126), -1.0, 0.0)),
    ).astype(BF16)

    @pl.loop(0, 16)
    def _(step):
        rows = pl.ds(pl.multiple_of(step * 32, 32), 32)

        def slab(ref, i):
            return ref[rows, 128 * i : 128 * i + 128]

        def cell(a, b):
            if a < 0:
                return slab(xlo, (a + 2) * 4 + b)
            if a > 3:
                return slab(xhi, (a - 4) * 4 + b)
            if b < 0:
                return slab(ylo, a * 2 + b + 2)
            if b > 3:
                return slab(yhi, a * 2 + b - 4)
            return slab(orb, a * 4 + b)

        for a in range(4):
            for b in range(4):
                center = cell(a, b)
                lap = bdot(center, circle)
                field = lambda i, j: cell(i, j).astype(F32)
                near = field(a - 1, b) + field(a + 1, b) + field(a, b - 1) + field(a, b + 1)
                far = field(a - 2, b) + field(a + 2, b) + field(a, b - 2) + field(a, b + 2)
                lap = lap + (16.0 * near - far)
                level = pot[4 * a + b : 4 * a + b + 1, :]
                value = lap * (-0.5 / 12.0) + level * center.astype(F32)
                hpsi[rows, 128 * (4 * a + b) : 128 * (4 * a + b) + 128] = value.astype(BF16)

    for t, (r, c) in enumerate(TILES_LOW):
        tile = bdot(hpsi[256 * r : 256 * r + 256, :], orb[256 * c : 256 * c + 256, :], NT)
        pay[2 * t] = tile[:, :128]
        pay[2 * t + 1] = tile[:, 128:]


def cross_kernel(orb, hpsi, other, pay):
    for m, left in enumerate((orb, hpsi)):
        for t, (r, c) in enumerate(TILES_ALL):
            tile = bdot(left[256 * r : 256 * r + 256, :], other[256 * c : 256 * c + 256, :], NT)
            pay[8 * m + 2 * t] = tile[:, :128]
            pay[8 * m + 2 * t + 1] = tile[:, 128:]


def rotate_kernel(rot_other, rot_own, other, own, out):
    for i in range(4):
        cols = slice(512 * i, 512 * i + 512)
        total = bdot(rot_own[...], own[:, cols]) + bdot(rot_other[...], other[:, cols])
        out[:, cols] = total.astype(BF16)


def shifted(piece, distance):
    n = lax.axis_size("domain")
    return lax.ppermute(piece, "domain", [((i - distance) % n, i) for i in range(n)])


def y_shift(piece, distance):
    n = lax.axis_size("domain")
    route = [((i // 8) * 8 + (i % 8 - distance) % 8, i) for i in range(n)]
    return lax.ppermute(piece, "domain", route)


def shards(orbitals, potential):
    orb = orbitals.reshape(HALF, CELLS)
    pot = potential.reshape(16, 128)
    other = lax.ppermute(orb, "band", [(0, 1)])
    xlo = shifted(orb[:, 1024:], 8)
    xhi = shifted(orb[:, :1024], -8)
    ylo = y_shift(jnp.concatenate([orb[:, 512 * a + 256 : 512 * a + 512] for a in range(4)], axis=1), 1)
    yhi = y_shift(jnp.concatenate([orb[:, 512 * a : 512 * a + 256] for a in range(4)], axis=1), -1)

    slab = lambda n: jax.ShapeDtypeStruct((n, 256, 128), F32)
    square = lambda n, t: jax.ShapeDtypeStruct((n, n), t)
    s_pay = call(own_overlap_kernel, slab(6), (orb, pot), "own_overlap", flops=2 * 10**9)
    (s_sum,) = all_sum(s_pay, None, 0, "sum_own_overlap")
    w0 = call(first_factor_kernel, square(512, F32), (s_sum,), "first_factor", flops=40 * 10**9)
    hpsi, h_pay = call(
        ham_kernel,
        [jax.ShapeDtypeStruct((HALF, CELLS), BF16), slab(6)],
        (orb, xlo, xhi, ylo, yhi, pot),
        "hamiltonian",
        flops=10 * 10**9,
    )
    cross = call(cross_kernel, slab(16), (orb, hpsi, other), "cross_overlap", flops=4 * 10**9)
    h_sum, cross_sum = all_sum(h_pay, cross, 1, "sum_rest")
    h_sub, rot_other, rot_own = call(
        last_kernel,
        [square(1024, F32), square(512, BF16), square(512, BF16)],
        (s_sum, h_sum, cross_sum, w0),
        "last_factor",
        scratch=[
            pltpu.VMEM((512, 1024), F32),
            pltpu.VMEM((512, 512), F32),
            pltpu.VMEM((1024, 1024), BF16),
            pltpu.VMEM((1024, 1024), BF16),
            pltpu.VMEM((1024, 1024), BF16),
            pltpu.VMEM((1024, 1024), BF16),
        ],
        flops=50 * 10**9,
    )
    rotated = call(
        rotate_kernel,
        jax.ShapeDtypeStruct((HALF, CELLS), BF16),
        (rot_other, rot_own, other, orb),
        "rotate",
        flops=4 * 10**9,
    )
    return rotated.reshape(orbitals.shape), h_sub


def solution(mesh):
    in_specs = (P("band", "domain", None), P("domain", None))
    out_specs = (P("band", "domain", None), P())
    return jax.shard_map(shards, mesh=mesh, in_specs=in_specs, out_specs=out_specs, check_vma=False)
```

time: 2320 us -> 312 us (0.13)
  waiting for transfers between devices: 1350 us -> 0.01 us
  other arithmetic: 389 us -> 0.25 us
  blocking collectives: 354 us -> 0 us
  Pallas kernels: 0 us -> 286 us
  matrix products: 101 us -> 0 us
  local copies, waits for them, and re-layouts: 76.8 us -> 6.83 us
    psum x1 -> x0, waiting for transfers between devices: 1310 us -> none  [shards(): s_summed, h_summed = lax.psum((s_rows, h_rows), 'domain')]
    psum x1 -> x0, blocking collectives: 354 us -> none  [shards(): pot_total = lax.psum(local_sum, 'domain')]
    pallas_call x0 -> x8, Pallas kernels: none -> 286 us  [call(): pl.pallas_call(kernel, out_shape=outs, in_specs=[VMEM] * len(args), out_s...]
    another operation x33 -> x0, other arithmetic: 256 us -> none  [the longest x30 172 us: shards(): chol = jnp.linalg.cholesky(intersection)]
    convert_element_type x65 -> x0, other arithmetic: 61.7 us -> none  [the longest x32 29.7 us: apply_padded(): yfield = ypad.astype(jnp.float32)]
    another operation x29 -> x0, matrix products: 51.5 us -> none  [the longest x15 28.4 us: shards(): lax.linalg.triangular_solve(chol, jnp.eye(total_orb, dtype=jnp.float32),...]
    dot_general x5 -> x0, matrix products: 49.6 us -> none  [the longest x1 20.3 us: shards(): jnp.dot(linv, ham, precision=lax.Precision.HIGHEST)]
    ppermute x7 -> x5, waiting for transfers between devices: 39.5 us -> 0.01 us  [the longest x2 0.01 us: y_shift(): return lax.ppermute(piece, 'domain', route)]
  transfers between devices with their start and end apart: 10 -> 5, of which waited for: 4 -> 0; matrix products, arithmetic and copies ran while one was open for 22% -> 1% of each run, Pallas kernels for 0% -> 53%
where the time goes in v1:
time: 312 us; the launch traced here: 310 us
  Pallas kernels  286 us (92%)
  starting transfers between devices  16.4 us (5%)
  local copies, waits for them, and re-layouts  6.83 us (2%)
    pallas_call x8, Pallas kernels, call(): pl.pallas_call(kernel, out_shape=outs, in_specs=[VMEM] * len(args), out_s...  286 us
    ppermute x1, starting transfers between devices, shards(): other = lax.ppermute(orb, 'band', [(0, 1)])  9.78 us
  transfers between devices with their start and end apart: 5, of which 0 were waited for; matrix products, arithmetic and copies ran while one was open for 1% of the time, Pallas kernels for 53%

profile of v1, /device:TPU:1, one launch (start us, length us, event | category | flops | bytes accessed | tf_op | source)
XLA Modules:
  0.0 310.5 jit_solution(11646125742929437429)
XLA Ops:
  0.6 9.8 %collective-permute-start.4 = (bf16[512,2048]{1,0:T(8,128)(2,1)}, bf16[512,2048]{1,0:T(8,128)(2,1)S(1)}, u32[]{:S(2)}, u32[]{:S(2)}) collective-permute-start(bf16[512,2048]{1,0:T(8,128)(2,1)} %bitcast.3), channel_id=1, source_target_pairs={{0,128},{1,129},{2,130},{3,131},{4,132},{5,133},{6,134},{7,135},{8... | collective-permute-start | bytes 6291464 | tf_op jit(solution)/shard_map/ppermute | solution.py:460
  10.4 1.7 fusion
  12.1 0.0 copy-start
  12.1 0.1 pad_maximum_fusion
  12.2 1.7 collective-permute-start.2
  13.9 0.1 pad_maximum_fusion.1
  14.0 0.0 copy-start.4
  14.0 0.1 collective-permute-start.3
  14.1 0.0 copy-done
  14.1 1.2 fusion.1
  15.3 4.9 %collective-permute-start.1 = (bf16[512,1024]{1,0:T(8,128)(2,1)}, bf16[512,1024]{1,0:T(8,128)(2,1)S(1)}, u32[]{:S(2)}, u32[]{:S(2)}) collective-permute-start(bf16[512,1024]{1,0:T(8,128)(2,1)} %get-tuple-element.24), channel_id=1, source_target_pairs={{8,0},{9,1},{10,2},{11,3},{12,4},{13,5},{14,6},{15,7},{16,8},{17,9... | collective-permute-start | bytes 3145736 | tf_op jit(solution)/shard_map/ppermute | solution.py:448
  20.2 0.0 collective-permute-start
  20.3 0.0 copy-done.4
  20.3 1.0 own_overlap.1.refs_0_
  21.3 121.3 %sum_own_overlap.1.s = f32[2,6,256,128]{3,2,1,0:T(8,128)S(1)} custom-call(f32[6,256,128]{2,1,0:T(8,128)S(1)} %own_overlap.1.refs_0_), custom_call_target="tpu_custom_call" | custom-call | flops 1000000000 | bytes 8388608 | tf_op jit(solution)/shard_map/sum_own_overlap/pallas_call | solution.py:38
  142.6 34.6 %first_factor.1.w0 = f32[512,512]{1,0:T(8,128)S(1)} custom-call(f32[2,6,256,128]{3,2,1,0:T(8,128)S(1)} %sum_own_overlap.1.s), custom_call_target="tpu_custom_call" | custom-call | flops 40000000000 | bytes 8388608 | tf_op jit(solution)/shard_map/first_factor/pallas_call | solution.py:38
  177.2 0.0 copy-start.1
  177.2 0.0 collective-permute-done.2.ylo
  177.2 0.0 collective-permute-done.3.yhi
  177.2 0.0 collective-permute-done.1.xhi
  177.2 0.0 collective-permute-done.xlo
  177.2 7.5 %hamiltonian.1 = (bf16[512,2048]{1,0:T(8,128)(2,1)}, f32[6,256,128]{2,1,0:T(8,128)S(1)}) custom-call(bf16[512,2048]{1,0:T(8,128)(2,1)} %bitcast.5, bf16[512,1024]{1,0:T(8,128)(2,1)S(1)} %collective-permute-done.xlo, bf16[512,1024]{1,0:T(8,128)(2,1)S(1)} %collective-permute-done.1.xhi, bf16[512,1024]{1,0:T(8,128)(2,1)S(1)} %collective-permute-done.2.ylo, ...), custom_call_target="tpu_custom_call" | custom-call | flops 10000000000 | bytes 8388608 | tf_op jit(solution)/shard_map/hamiltonian/pallas_call | solution.py:38
  184.7 0.0 collective-permute-done.4.other
  184.7 0.0 copy-start.2
  184.7 1.3 copy-done.2
  186.0 0.0 copy-done.1
  186.0 4.6 %cross_overlap.1.refs_1_ = f32[16,256,128]{2,1,0:T(8,128)S(1)} custom-call(bf16[512,2048]{1,0:T(8,128)(2,1)S(1)} %bitcast.8, bf16[512,2048]{1,0:T(8,128)(2,1)} %get-tuple-element.10.hpsi, bf16[512,2048]{1,0:T(8,128)(2,1)} %copy-done.2), custom_call_target="tpu_custom_call" | custom-call | flops 4000000000 | bytes 8388608 | tf_op jit(solution)/shard_map/cross_overlap/pallas_call | solution.py:38
  190.6 0.0 copy-start.6
  190.6 1.3 copy-done.6
  191.9 62.2 %sum_rest.1 = (f32[2,6,256,128]{3,2,1,0:T(8,128)S(1)}, f32[16,256,128]{2,1,0:T(8,128)S(1)}) custom-call(f32[6,256,128]{2,1,0:T(8,128)S(1)} %get-tuple-element.9.refs_0_, f32[16,256,128]{2,1,0:T(8,128)} %copy-done.6), custom_call_target="tpu_custom_call" | custom-call | flops 1000000000 | bytes 8388608 | tf_op jit(solution)/shard_map/sum_rest/pallas_call | solution.py:38
  254.1 0.0 copy-start.5
  254.1 1.3 copy-done.5
  255.4 0.0 copy-start.3
  255.4 51.4 %last_factor.1 = (f32[1024,1024]{1,0:T(8,128)}, bf16[512,512]{1,0:T(8,128)(2,1)S(1)}, bf16[512,512]{1,0:T(8,128)(2,1)S(1)}) custom-call(f32[2,6,256,128]{3,2,1,0:T(8,128)S(1)} %sum_own_overlap.1.s, f32[2,6,256,128]{3,2,1,0:T(8,128)S(1)} %get-tuple-element.11.hown, f32[16,256,128]{2,1,0:T(8,128)} %copy-done.5, f32[512,512]{1,0:T(8,128)S(1)} %first_factor.1.w0), custom_call_target="tpu_custom_call" | custom-call | flops 49999998976 | bytes 8388608 | tf_op jit(solution)/shard_map/last_factor/pallas_call | solution.py:38
  306.8 0.0 copy-done.3
  306.8 3.7 %rotate.1 = bf16[512,2048]{1,0:T(8,128)(2,1)} custom-call(bf16[512,512]{1,0:T(8,128)(2,1)S(1)} %get-tuple-element.13.rot_other, bf16[512,512]{1,0:T(8,128)(2,1)S(1)} %get-tuple-element.14.rot_own, bf16[512,2048]{1,0:T(8,128)(2,1)S(1)} %copy-done.3, bf16[512,2048]{1,0:T(8,128)(2,1)S(1)} %bitcast.9), custom_call_target="tpu_custom_call" | custom-call | flops 4000000000 | bytes 8388608 | tf_op jit(solution)/shard_map/rotate/pallas_call | solution.py:38
Async XLA Ops:
  0.6 184.1 %collective-permute-start.4 = (bf16[512,2048]{1,0:T(8,128)(2,1)}, bf16[512,2048]{1,0:T(8,128)(2,1)S(1)}, u32[]{:S(2)}, u32[]{:S(2)}) collective-permute-start(bf16[512,2048]{1,0:T(8,128)(2,1)} %bitcast.3), channel_id=1, source_target_pairs={{0,128},{1,129},{2,130},{3,131},{4,132},{5,133},{6,134},{7,135},{8... | collective-permute-start | bytes 6291464 | tf_op jit(solution)/shard_map/ppermute | solution.py:460
  12.1 2.0 copy-start
  12.2 165.0 %collective-permute-start.2 = (bf16[512,1024]{1,0:T(8,128)(2,1)S(1)}, bf16[512,1024]{1,0:T(8,128)(2,1)S(1)}, u32[]{:S(2)}, u32[]{:S(2)}) collective-permute-start(bf16[512,1024]{1,0:T(8,128)(2,1)S(1)} %pad_maximum_fusion), channel_id=1, source_target_pairs={{7,0},{0,1},{1,2},{2,3},{3,4},{4,5},{5,6},{6,7},{15,8},{8,9},{9,10... | collective-permute-start | bytes 3145736 | tf_op jit(solution)/shard_map/ppermute | solution.py:454
  14.0 6.2 %copy-start.4 = (f32[1,2048]{1,0:T(1,128)S(1)}, f32[1,2048]{1,0:T(1,128)}, u32[]{:S(2)}) copy-start(f32[1,2048]{1,0:T(1,128)} %param.3) | copy-start | bytes 24580
  14.0 163.2 %collective-permute-start.3 = (bf16[512,1024]{1,0:T(8,128)(2,1)S(1)}, bf16[512,1024]{1,0:T(8,128)(2,1)S(1)}, u32[]{:S(2)}, u32[]{:S(2)}) collective-permute-start(bf16[512,1024]{1,0:T(8,128)(2,1)S(1)} %pad_maximum_fusion.1), channel_id=1, source_target_pairs={{1,0},{2,1},{3,2},{4,3},{5,4},{6,5},{7,6},{0,7},{9,8},{10,9},{11,1... | collective-permute-start | bytes 3145736 | tf_op jit(solution)/shard_map/ppermute | solution.py:454
  15.3 161.9 %collective-permute-start.1 = (bf16[512,1024]{1,0:T(8,128)(2,1)}, bf16[512,1024]{1,0:T(8,128)(2,1)S(1)}, u32[]{:S(2)}, u32[]{:S(2)}) collective-permute-start(bf16[512,1024]{1,0:T(8,128)(2,1)} %get-tuple-element.24), channel_id=1, source_target_pairs={{8,0},{9,1},{10,2},{11,3},{12,4},{13,5},{14,6},{15,7},{16,8},{17,9... | collective-permute-start | bytes 3145736 | tf_op jit(solution)/shard_map/ppermute | solution.py:448
  20.2 157.0 %collective-permute-start = (bf16[512,1024]{1,0:T(8,128)(2,1)S(1)}, bf16[512,1024]{1,0:T(8,128)(2,1)S(1)}, u32[]{:S(2)}, u32[]{:S(2)}) collective-permute-start(bf16[512,1024]{1,0:T(8,128)(2,1)S(1)} %get-tuple-element.25), channel_id=1, source_target_pairs={{120,0},{121,1},{122,2},{123,3},{124,4},{125,5},{126,6},{127,7},{0... | collective-permute-start | bytes 3145736 | tf_op jit(solution)/shard_map/ppermute | solution.py:448
  177.2 8.8 %copy-start.1 = (bf16[512,1,2048]{2,0,1:T(8,128)(2,1)S(1)}, bf16[512,1,2048]{2,0,1:T(8,128)(2,1)}, u32[]{:S(2)}) copy-start(bf16[512,1,2048]{2,0,1:T(8,128)(2,1)} %param.2) | copy-start | bytes 6291460
  184.7 1.3 copy-start.2
  190.6 1.3 copy-start.6
  254.1 1.3 copy-start.5
  255.4 51.4 %copy-start.3 = (bf16[512,2048]{1,0:T(8,128)(2,1)S(1)}, bf16[512,2048]{1,0:T(8,128)(2,1)}, u32[]{:S(2)}) copy-start(bf16[512,2048]{1,0:T(8,128)(2,1)} %copy-done.2) | copy-start | bytes 6291460

commit v2 on v1

v2 whole, which is shorter than its diff:
```python
import jax
import jax.numpy as jnp
from jax import lax
from jax.experimental import pallas as pl
from jax.experimental.pallas import tpu as pltpu
from jax.sharding import PartitionSpec as P

MESH = pl.DeviceIdType.MESH
HI = lax.Precision.HIGHEST
NN = (((1,), (0,)), ((), ()))
NT = (((1,), (1,)), ((), ()))
TN = (((0,), (0,)), ((), ()))
F32 = jnp.float32
BF16 = jnp.bfloat16
VMEM = pl.BlockSpec(memory_space=pltpu.VMEM)
ANY = pl.BlockSpec(memory_space=pl.ANY)
MIB = 2**20
CELLS = 2048
HALF = 512
TILES_UP = ((0, 0), (0, 1), (1, 1))
TILES_LOW = ((0, 0), (1, 0), (1, 1))
TILES_ALL = ((0, 0), (0, 1), (1, 0), (1, 1))


def fdot(a, b, dims=NN):
    return lax.dot_general(a, b, dims, precision=HI, preferred_element_type=F32)


def bdot(a, b, dims=NN):
    return lax.dot_general(a, b, dims, preferred_element_type=F32)


def call(kernel, outs, args, name, scratch=(), collective=None, limit=48, flops=0, far_in=(), far_out=()):
    params = dict(vmem_limit_bytes=limit * MIB)
    if collective is not None:
        params.update(collective_id=collective, has_side_effects=True)
    return pl.pallas_call(
        kernel,
        out_shape=outs,
        in_specs=[ANY if i in far_in else VMEM for i in range(len(args))],
        out_specs=[ANY if i in far_out else VMEM for i in range(len(outs))],
        scratch_shapes=list(scratch),
        compiler_params=pltpu.CompilerParams(**params),
        cost_estimate=pl.CostEstimate(flops=flops, bytes_accessed=8 * MIB, transcendentals=0),
        name=name,
    )(*args)


def packers(lower):
    z = lax.broadcasted_iota(jnp.int32, (128, 128), 0)
    lane = lax.broadcasted_iota(jnp.int32, (128, 128), 1)
    even = (lane < 64) & (z == lane + lower)
    odd = (lane >= 64) & (z == lane - 64 + lower)
    return even.astype(F32).astype(BF16), odd.astype(F32).astype(BF16)


def edge_cells():
    lane = lax.broadcasted_iota(jnp.int32, (128, 128), 1)
    q = lane % 4
    return lane // 4, jnp.where(q < 2, 64 + q, 124 + q)


def pack_kernel(orb, pot, pay, send, keep):
    band = lax.axis_index("band")
    for t, (r, c) in enumerate(TILES_UP):
        tile = bdot(orb[256 * r : 256 * r + 256, :], orb[256 * c : 256 * c + 256, :], NT)
        pay[2 * t] = tile[:, :128]
        pay[2 * t + 1] = tile[:, 128:]
    pay[0, 128:136, :] = pot[0:8, :] + pot[8:16, :]
    z = lax.broadcasted_iota(jnp.int32, (128, 128), 0)
    owner, level = edge_cells()

    @pl.loop(0, 4)
    def _(step):
        rows = pl.ds(pl.multiple_of(step * 128, 128), 128)
        slab = lambda i: orb[rows, 128 * i : 128 * i + 128]
        for ref, lower in ((send, 64 * band), (keep, 64 - 64 * band)):
            even, odd = packers(lower)
            for m in range(8):
                packed = bdot(slab(2 * m), even) + bdot(slab(2 * m + 1), odd)
                ref[rows, 128 * m : 128 * m + 128] = packed.astype(BF16)
        edge = jnp.zeros((128, 128), F32)
        for i in range(16):
            pick = ((owner == i) & (z == level)).astype(F32).astype(BF16)
            edge = edge + bdot(slab(i), pick)
        send[rows, 1024:1152] = edge.astype(BF16)


class Place:
    def __init__(self):
        self.band = lax.axis_index("band")
        dom = lax.axis_index("domain")
        self.x, self.y = dom // 32, (dom // 8) % 4
        self.z, self.core = (dom // 2) % 4, dom % 2
        self.here = self.x * 4 + self.y
        self.zz = self.band * 4 + self.z
        self.partner = self.at(self.band, self.x, self.y, self.z, 1 - self.core)
        self.opposite = (1 - self.band, dom)
        self.next_x = (self.band, (dom + 8) % 128)
        self.last_x = (self.band, (dom + 120) % 128)
        self.next_y = (self.band, (dom // 8) * 8 + (dom + 1) % 8)
        self.last_y = (self.band, (dom // 8) * 8 + (dom + 7) % 8)

    @staticmethod
    def at(b, xx, yy, zl, cc):
        return (b, ((xx * 4 + yy) * 4 + zl) * 2 + cc)

    def xy_peer(self, k):
        xx, yy = (self.x + k // 4) % 4, (self.y + k % 4) % 4
        return self.at(self.band, xx, yy, self.z, self.core), xx * 4 + yy

    def xy_source(self, k):
        return ((self.x + 4 - k // 4) % 4) * 4 + (self.y + 4 - k % 4) % 4

    def z_peer(self, k):
        other = (self.zz + k) % 8
        return self.at(other // 4, self.x, self.y, other % 4, self.core)

    def greet(self, y_too):
        barrier = pltpu.get_barrier_semaphore()
        peers = [self.partner]
        peers += [self.xy_peer(k)[0] for k in range(1, 16)]
        peers += [self.z_peer(k) for k in range(1, 8)]
        if y_too:
            band, dom = self.next_y
            peers.append((band, jnp.where(self.core == 0, self.last_y[1], dom)))
        for peer in peers:
            pl.semaphore_signal(barrier, inc=1, device_id=peer, device_id_type=MESH)
        pl.semaphore_wait(barrier, len(peers))


def remote(src, dst, send, recv, device):
    return pltpu.make_async_remote_copy(
        src_ref=src, dst_ref=dst, send_sem=send, recv_sem=recv, device_id=device, device_id_type=MESH
    )


class Bulk:
    def __init__(self, pieces, device, sems, first, condition=None, other=None):
        self.sems, self.first, self.device = sems, first, device
        self.pieces, self.condition, self.other = pieces, condition, other
        self.started = 0

    def copy(self, i):
        src, dst = self.pieces[i]
        return remote(src, dst, self.sems[0].at[self.first + i], self.sems[1].at[self.first + i], self.device)

    def start(self, count=None):
        stop = len(self.pieces) if count is None else self.started + count

        def body():
            for i in range(self.started, stop):
                self.copy(i).start()

        if self.condition is None:
            body()
        else:
            pl.when(self.condition)(body)
        self.started = stop

    def wait(self):
        if self.condition is None:
            for i in range(len(self.pieces)):
                self.copy(i).wait()
            return

        @pl.when(self.condition)
        def _():
            for i in range(len(self.pieces)):
                self.copy(i).wait_send()

        @pl.when(self.other)
        def _():
            for i in range(len(self.pieces)):
                self.copy(i).wait_recv()


class Sum:
    scratch_count = 4 + 10

    def __init__(self, place, both, pay, out, scratch):
        self.place, self.both, self.pay, self.out = place, both, pay, out
        self.half, self.whole, self.got, self.along = scratch[:4]
        self.s1, self.r1, self.s2, self.r2, self.s3, self.r3, self.s4, self.r4, self.s5, self.r5 = scratch[4:14]

    @staticmethod
    def scratch(n):
        dma = pltpu.SemaphoreType.DMA
        return [
            pltpu.VMEM((n, 128, 128), F32),
            pltpu.VMEM((n, 128, 128), F32),
            pltpu.VMEM((16, n, 8, 128), F32),
            pltpu.VMEM((8, n, 8, 128), F32),
            dma((1,)),
            dma((1,)),
            dma((16,)),
            dma((16,)),
            dma((8,)),
            dma((8,)),
            dma((16,)),
            dma((16,)),
            dma((16,)),
            dma((16,)),
        ]

    def first(self):
        p = self.place
        theirs = pl.ds(pl.multiple_of((1 - p.core) * 128, 128), 128)
        return remote(self.pay.at[:, theirs, :], self.half, self.s1.at[0], self.r1.at[0], p.partner)

    def second(self, k):
        device, there = self.place.xy_peer(k)
        rows = pl.ds(pl.multiple_of(there * 8, 8), 8)
        return remote(self.whole.at[:, rows, :], self.got.at[k], self.s2.at[k], self.r2.at[k], device)

    def third(self, k):
        p = self.place
        return remote(self.along.at[p.zz], self.along.at[p.zz], self.s3.at[k], self.r3.at[k], p.z_peer(k))

    def spot(self, row):
        rows = pl.ds(pl.multiple_of(self.place.core * 128 + row * 8, 8), 8)
        return self.out.at[:, :, rows, :] if self.both else self.out.at[:, rows, :]

    def fourth(self, k, row):
        spot = self.spot(row)
        return remote(spot, spot, self.s4.at[k], self.r4.at[k], self.place.xy_peer(k)[0])

    def fifth(self, k, row):
        spot = self.spot(row)
        return remote(spot, spot, self.s5.at[k], self.r5.at[k], self.place.partner)

    def part1(self):
        self.first().start()

    def part2(self):
        self.first().wait()
        mine = pl.ds(pl.multiple_of(self.place.core * 128, 128), 128)
        self.whole[...] = self.pay[:, mine, :] + self.half[...]
        for k in range(1, 16):
            self.second(k).start()

    def part3(self):
        p = self.place
        for k in range(1, 16):
            self.second(k).wait()
        total = self.whole[:, pl.ds(pl.multiple_of(p.here * 8, 8), 8), :]
        for k in range(1, 16):
            total = total + self.got[k]
        self.along[p.zz] = total
        for k in range(1, 8):
            self.third(k).start()

    def part4(self):
        p = self.place
        for k in range(1, 8):
            self.third(k).wait()
        along = self.along
        lower = along[0] + along[1] + along[2] + along[3]
        upper = along[4] + along[5] + along[6] + along[7]
        rows = pl.ds(pl.multiple_of(p.core * 128 + p.here * 8, 8), 8)
        if self.both:
            self.out[0, :, rows, :] = lower
            self.out[1, :, rows, :] = upper
        else:
            self.out[:, rows, :] = lower + upper
        for k in range(1, 16):
            self.fourth(k, p.here).start()
        self.fifth(0, p.here).start()

    def part5(self):
        p = self.place
        for k in range(1, 16):
            source = p.xy_source(k)
            self.fourth(k, source).wait_recv()
            self.fifth(k, source).start()

    def end(self):
        p = self.place
        for k in range(1, 16):
            self.fourth(k, p.here).wait_send()
        for k in range(16):
            self.fifth(k, p.here).wait()


def invert_block(block):
    lane = lax.broadcasted_iota(jnp.int32, (8, 128), 1)
    sub = lax.broadcasted_iota(jnp.int32, (8, 128), 0)
    rows = [block[8 * p : 8 * p + 8] for p in range(16)]
    for p in range(16):
        k = 8 * p
        panel = rows[p]
        d = [[jnp.broadcast_to(panel[i : i + 1, k + j : k + j + 1], (8, 128)) for j in range(i + 1)] for i in range(8)]
        inside = (lane >= k) & (lane < k + 8)
        start = jnp.where(inside, (lane == k + sub).astype(F32), panel)
        acc = [jnp.broadcast_to(start[s : s + 1, :], (8, 128)) for s in range(8)]
        done = []
        for j in range(8):
            r = lax.rsqrt(d[j][j])
            xj = acc[j] * r
            done.append(xj)
            low = [None] * 8
            for i in range(j + 1, 8):
                low[i] = d[i][j] * r
            for i in range(j + 1, 8):
                for m in range(j + 1, i + 1):
                    d[i][m] = d[i][m] - low[i] * low[m]
                acc[i] = acc[i] - low[i] * xj
        x = done[0]
        for s in range(1, 8):
            x = jnp.where(sub == s, done[s], x)
        rows[p] = x
        if p < 15:
            right = jnp.where(lane >= k + 8, x, 0.0)
            update = fdot(right, x, TN)
            for q in range(p + 1, 16):
                rows[q] = jnp.where(inside, 0.0, rows[q]) - update[8 * q : 8 * q + 8]
    whole = jnp.concatenate(rows, axis=0)
    rr = lax.broadcasted_iota(jnp.int32, (128, 128), 0)
    cc = lax.broadcasted_iota(jnp.int32, (128, 128), 1)
    return jnp.where(cc <= rr, whole, 0.0)


def eliminate_step(c, offset, j):
    blocks = c.shape[0] // 128
    rr = lax.broadcasted_iota(jnp.int32, (128, 128), 0)
    cc = lax.broadcasted_iota(jnp.int32, (128, 128), 1)
    rows, cols = slice(128 * j, 128 * j + 128), slice(offset + 128 * j, offset + 128 * j + 128)
    inverse = invert_block(c[rows, cols])
    c[rows, cols] = (rr == cc).astype(F32)
    c[rows, :] = fdot(inverse, c[rows, :])
    for i in range(j + 1, blocks):
        below = slice(128 * i, 128 * i + 128)
        across = slice(offset + 128 * i, offset + 128 * i + 128)
        factor = c[rows, across]
        c[below, cols] = jnp.zeros((128, 128), F32)
        c[below, :] = c[below, :] - fdot(factor, c[rows, :], TN)


def clear_right(c, offset):
    for i in range(c.shape[0] // 128):
        for j in range(i + 1, c.shape[0] // 128):
            c[128 * i : 128 * i + 128, offset + 128 * j : offset + 128 * j + 128] = jnp.zeros((128, 128), F32)


def spread(c, slabs, tiles, offset):
    for t, (r, col) in enumerate(tiles):
        for h in range(2):
            lo = offset + 256 * col + 128 * h
            c[256 * r : 256 * r + 256, lo : lo + 128] = slabs(2 * t + h)


def swap_kernel(pay, orb, send, s_sum, recv, xlo, xhi, *scratch):
    place = Place()
    total = Sum(place, True, pay, s_sum, scratch[:14])
    sems = scratch[14:16]
    rows = lambda n, i: pl.ds((HALF // n) * i, HALF // n)
    swap = Bulk([(send.at[rows(8, i), :], recv.at[rows(8, i), :]) for i in range(8)], place.opposite, sems, 0)
    up = Bulk(
        [(orb.at[rows(4, i), pl.ds(1024, 1024)], xlo.at[rows(4, i), :]) for i in range(4)], place.next_x, sems, 8
    )
    down = Bulk(
        [(orb.at[rows(4, i), pl.ds(0, 1024)], xhi.at[rows(4, i), :]) for i in range(4)], place.last_x, sems, 12
    )
    place.greet(False)
    total.part1()
    swap.start(2)
    total.part2()
    up.start()
    down.start()
    total.part3()
    swap.start()
    total.part4()
    total.part5()
    total.end()
    up.wait()
    down.wait()
    swap.wait()


def first_factor_kernel(s, pay, orb, x_sum, w, ylo, yhi, *scratch):
    place = Place()
    total = Sum(place, False, pay, x_sum, scratch[:14])
    sems = scratch[14:16]
    up = Bulk(
        [(orb.at[:, pl.ds(512 * a + 256, 256)], ylo.at[:, pl.ds(256 * a, 256)]) for a in range(4)],
        place.next_y,
        sems,
        0,
    )
    down = Bulk(
        [(orb.at[:, pl.ds(512 * a, 256)], yhi.at[:, pl.ds(256 * a, 256)]) for a in range(4)], place.last_y, sems, 4
    )
    place.greet(True)
    total.part1()
    w[256:512, 0:256] = jnp.zeros((256, 256), F32)
    spread(w, lambda i: s[0, i], TILES_UP, 0)
    total.part2()
    eliminate_step(w, 0, 0)
    total.part3()
    up.start()
    down.start()
    eliminate_step(w, 0, 1)
    total.part4()
    eliminate_step(w, 0, 2)
    total.part5()
    eliminate_step(w, 0, 3)
    clear_right(w, 0)
    total.end()
    up.wait()
    down.wait()


def second_factor_kernel(s, x, w0, hown, hcross, keep, c, hown_sum, hcross_sum, rest, *scratch):
    place = Place()
    own = Sum(place, True, hown, hown_sum, scratch[:14])
    cross = Sum(place, False, hcross, hcross_sum, scratch[14:28])
    sems = scratch[28:30]
    cross_s = scratch[30]
    rows = lambda i: pl.ds(64 * i, 64)
    tail = Bulk(
        [(keep.at[rows(i), :], rest.at[rows(i), :]) for i in range(8)],
        place.opposite,
        sems,
        0,
        place.band == 0,
        place.band == 1,
    )
    place.greet(False)
    own.part1()
    cross.part1()
    for t, (r, col) in enumerate(TILES_ALL):
        for h in range(2):
            lo = 256 * col + 128 * h
            cross_s[256 * r : 256 * r + 256, lo : lo + 128] = x[2 * t + h]
    low = fdot(cross_s[...], w0[...], NT)
    c[256:512, 512:768] = jnp.zeros((256, 256), F32)
    spread(c, lambda i: s[1, i], TILES_UP, 512)
    c[:, 512:1024] = c[:, 512:1024] - fdot(low, low, NT)
    c[:, 0:512] = -fdot(low, w0[...])
    own.part2()
    cross.part2()
    eliminate_step(c, 512, 0)
    own.part3()
    cross.part3()
    tail.start()
    eliminate_step(c, 512, 1)
    own.part4()
    cross.part4()
    eliminate_step(c, 512, 2)
    own.part5()
    cross.part5()
    eliminate_step(c, 512, 3)
    clear_right(c, 512)
    own.end()
    cross.end()
    tail.wait()


def split(a):
    high = a.astype(BF16)
    return high, (a - high.astype(F32)).astype(BF16)


def dot3(a, b, dims=NN):
    return bdot(a[0], b[0], dims) + (bdot(a[0], b[1], dims) + bdot(a[1], b[0], dims))


def last_kernel(s, hown, cross, w0, c, h_sub, rot_other, rot_own, wh, wl, mh, ml):
    band = lax.axis_index("band")

    @pl.when(band == 0)
    def _():
        rot_own[...] = w0[...].astype(BF16)
        rot_other[...] = jnp.zeros((512, 512), BF16)

    @pl.when(band == 1)
    def _():
        rot_own[...] = c[:, 512:1024].astype(BF16)
        rot_other[...] = c[:, 0:512].astype(BF16)

    for r in range(4):
        source = w0 if r < 2 else c
        base = 256 * (r % 2)
        width = 512 if r < 2 else 1024
        high, lowpart = split(source[base : base + 256, :])
        wh[256 * r : 256 * r + 256, 0:width] = high
        wl[256 * r : 256 * r + 256, 0:width] = lowpart

    rr = lax.broadcasted_iota(jnp.int32, (256, 256), 0)
    cc = lax.broadcasted_iota(jnp.int32, (256, 256), 1)
    weight = jnp.where(cc < rr, 1.0, jnp.where(cc == rr, 0.5, 0.0)).astype(F32)

    def pair(slabs, t):
        return jnp.concatenate([slabs(2 * t), slabs(2 * t + 1)], axis=1)

    half = {}
    for b in range(2):
        for t, (r, col) in enumerate(TILES_LOW):
            tile = pair(lambda i: hown[b, i], t)
            if r == col:
                tile = tile * weight
            half[2 * b + r, 2 * b + col] = split(tile)
    for t, (r, col) in enumerate(TILES_ALL):
        half[2 + r, col] = split(pair(lambda i: cross[i], t))

    def block(high, lowpart, r, col):
        rows, cols = slice(256 * r, 256 * r + 256), slice(256 * col, 256 * col + 256)
        return high[rows, cols], lowpart[rows, cols]

    for r in range(4):
        for col in range(r + 1):
            total = None
            for k in range(col, r + 1):
                part = dot3(block(wh, wl, r, k), half[k, col])
                total = part if total is None else total + part
            high, lowpart = split(total)
            mh[256 * r : 256 * r + 256, 256 * col : 256 * col + 256] = high
            ml[256 * r : 256 * r + 256, 256 * col : 256 * col + 256] = lowpart

    vmean = jnp.sum(s[0, 0, 128:136, :]) / (128 * CELLS)
    shift = jnp.where(rr == cc, vmean, 0.0)

    def product(r, col):
        total = None
        for k in range(min(r, col) + 1):
            part = dot3(block(mh, ml, r, k), block(wh, wl, col, k), NT)
            total = part if total is None else total + part
        return total

    for r in range(4):
        for col in range(r + 1):
            tile = product(r, col)
            if r == col:
                h_sub[256 * r : 256 * r + 256, 256 * r : 256 * r + 256] = tile + tile.T - shift
            else:
                tile = tile + product(col, r).T
                h_sub[256 * r : 256 * r + 256, 256 * col : 256 * col + 256] = tile
                h_sub[256 * col : 256 * col + 256, 256 * r : 256 * r + 256] = tile.T


def circle_weights():
    row = lax.broadcasted_iota(jnp.int32, (128, 128), 0)
    col = lax.broadcasted_iota(jnp.int32, (128, 128), 1)
    return row, col, step_weights((row - col + 128) % 128)


def step_weights(away):
    near = (away == 1) | (away == 127)
    far = (away == 2) | (away == 126)
    return jnp.where(near, 16.0, jnp.where(far, -1.0, 0.0))


def ham_kernel(orb, xlo, xhi, ylo, yhi, pot, recv, pay, cross, hpsi, half, edge):
    band = lax.axis_index("band")
    row, col, weights = circle_weights()
    full = jnp.where(row == col, -90.0, weights)
    inner = jnp.where((band == 1) | ((row >= 64) & (col >= 64)), full, 0.0)
    full, inner = full.astype(BF16), inner.astype(BF16)
    owner, level = edge_cells()
    even, odd = packers(64 - 64 * band)

    @pl.loop(0, 16)
    def _(step):
        rows = pl.ds(pl.multiple_of(step * 32, 32), 32)

        def slab(ref, i):
            return ref[rows, 128 * i : 128 * i + 128]

        def cell(a, b):
            if a < 0:
                return slab(xlo, (a + 2) * 4 + b)
            if a > 3:
                return slab(xhi, (a - 4) * 4 + b)
            if b < 0:
                return slab(ylo, a * 2 + b + 2)
            if b > 3:
                return slab(yhi, a * 2 + b - 4)
            return slab(orb, a * 4 + b)

        for pair in range(8):
            packed = None
            for i in (2 * pair, 2 * pair + 1):
                a, b = i // 4, i % 4
                center = cell(a, b)
                field = lambda i, j: cell(i, j).astype(F32)
                near = field(a - 1, b) + field(a + 1, b) + field(a, b - 1) + field(a, b + 1)
                far = field(a - 2, b) + field(a + 2, b) + field(a, b - 2) + field(a, b + 2)
                across = 16.0 * near - far
                base = pot[i : i + 1, :] * center.astype(F32)
                value = (across + bdot(center, full)) * (-0.5 / 12.0) + base
                hpsi[rows, 128 * i : 128 * i + 128] = value.astype(BF16)
                value = (across + bdot(center, inner)) * (-0.5 / 12.0) + base
                part = bdot(value.astype(BF16), even if i % 2 == 0 else odd)
                packed = part if packed is None else packed + part
            half[rows, 128 * pair : 128 * pair + 128] = packed.astype(BF16)

    @pl.loop(0, 4)
    def _(step):
        rows = pl.ds(pl.multiple_of(step * 128, 128), 128)
        total = jnp.zeros((128, 128), F32)
        for i in range(16):
            weight = jnp.where((owner == i) & (row < 64), step_weights((row - level + 128) % 128), 0.0)
            total = total + bdot(orb[rows, 128 * i : 128 * i + 128], weight.astype(BF16))
        edge[rows, :] = jnp.where(band == 1, total * (-0.5 / 12.0), 0.0).astype(BF16)

    for t, (r, c) in enumerate(TILES_LOW):
        tile = bdot(hpsi[256 * r : 256 * r + 256, :], orb[256 * c : 256 * c + 256, :], NT)
        pay[2 * t] = tile[:, :128]
        pay[2 * t + 1] = tile[:, 128:]
    cross_products(band, half, recv, cross, edge)


def cross_products(band, half, recv, out, edge=None):
    def products(left, right, corner):
        for t, (r, c) in enumerate(TILES_ALL):
            up, across = slice(256 * r, 256 * r + 256), slice(256 * c, 256 * c + 256)
            tile = bdot(left[up, 0:1024], right[across, 0:1024], NT)
            if corner:
                tile = tile + bdot(edge[up, :], recv[across, 1024:1152], NT)
            out[2 * t] = tile[:, :128]
            out[2 * t + 1] = tile[:, 128:]

    @pl.when(band == 1)
    def _():
        products(half, recv, edge is not None)

    @pl.when(band == 0)
    def _():
        products(recv, half, False)


def cross_kernel(keep, recv, out):
    cross_products(lax.axis_index("band"), keep, recv, out)


def rotate_kernel(rot_other, rot_own, recv, rest, own, out):
    band = lax.axis_index("band")

    @pl.when(band == 0)
    def _():
        for i in range(4):
            there = slice(512 * i, 512 * i + 512)
            out[:, there] = bdot(rot_own[...], own[:, there]).astype(BF16)

    @pl.when(band == 1)
    def _():
        low_even, low_odd = packers(0)
        high_even, high_odd = packers(64)
        for m in range(8):
            cols = slice(128 * m, 128 * m + 128)
            low, high = recv[:, cols], rest[:, cols]
            even = (bdot(low, low_even, NT) + bdot(high, high_even, NT)).astype(BF16)
            odd = (bdot(low, low_odd, NT) + bdot(high, high_odd, NT)).astype(BF16)
            other = jnp.concatenate([even, odd], axis=1)
            there = slice(256 * m, 256 * m + 256)
            total = bdot(rot_own[...], own[:, there]) + bdot(rot_other[...], other)
            out[:, there] = total.astype(BF16)


def shards(orbitals, potential):
    orb = orbitals.reshape(HALF, CELLS)
    pot = potential.reshape(16, 128)
    slab = lambda n: jax.ShapeDtypeStruct((n, 256, 128), F32)
    square = lambda n, t: jax.ShapeDtypeStruct((n, n), t)
    wide = lambda n: jax.ShapeDtypeStruct((HALF, n), BF16)
    two = lambda n: jax.ShapeDtypeStruct((2, n, 256, 128), F32)
    dma = pltpu.SemaphoreType.DMA
    s_pay, send, keep = call(pack_kernel, [slab(6), wide(1152), wide(1024)], (orb, pot), "pack")
    s_sum, recv, xlo, xhi = call(
        swap_kernel,
        [two(6), wide(1152), wide(1024), wide(1024)],
        (s_pay, orb, send),
        "swap_and_sum",
        scratch=Sum.scratch(6) + [dma((16,)), dma((16,))],
        collective=0,
        far_in=(1, 2),
        far_out=(1, 2, 3),
    )
    (x_pay,) = call(cross_kernel, [slab(8)], (keep, recv), "cross_overlap")
    x_sum, w0, ylo, yhi = call(
        first_factor_kernel,
        [slab(8), square(512, F32), wide(1024), wide(1024)],
        (s_sum, x_pay, orb),
        "first_factor",
        scratch=Sum.scratch(8) + [dma((8,)), dma((8,))],
        collective=1,
        far_in=(2,),
        far_out=(2, 3),
    )
    h_pay, hx_pay = call(
        ham_kernel,
        [slab(6), slab(8)],
        (orb, xlo, xhi, ylo, yhi, pot, recv),
        "hamiltonian",
        scratch=[pltpu.VMEM((HALF, CELLS), BF16), pltpu.VMEM((HALF, 1024), BF16), pltpu.VMEM((HALF, 128), BF16)],
    )
    c, h_sum, hx_sum, rest = call(
        second_factor_kernel,
        [jax.ShapeDtypeStruct((HALF, 1024), F32), two(6), slab(8), wide(1024)],
        (s_sum, x_sum, w0, h_pay, hx_pay, keep),
        "second_factor",
        scratch=Sum.scratch(6) + Sum.scratch(8) + [dma((8,)), dma((8,)), pltpu.VMEM((512, 512), F32)],
        collective=2,
        far_in=(5,),
        far_out=(3,),
    )
    h_sub, rot_other, rot_own = call(
        last_kernel,
        [square(1024, F32), square(512, BF16), square(512, BF16)],
        (s_sum, h_sum, hx_sum, w0, c),
        "subspace_matrix",
        scratch=[pltpu.VMEM((1024, 1024), BF16)] * 4,
    )
    (rotated,) = call(rotate_kernel, [wide(CELLS)], (rot_other, rot_own, recv, rest, orb), "rotate")
    return rotated.reshape(orbitals.shape), h_sub


def solution(mesh):
    in_specs = (P("band", "domain", None), P("domain", None))
    out_specs = (P("band", "domain", None), P())
    return jax.shard_map(shards, mesh=mesh, in_specs=in_specs, out_specs=out_specs, check_vma=False)
```

time: 312 us -> 247 us (0.79)
  the two profiles are of different devices: /device:TPU:1 before, /device:TPU:193 now
where the time goes in v2:
time: 247 us; the launch traced here: 243 us
  Pallas kernels  240 us (97%)
    pallas_call x8, Pallas kernels, call(): pl.pallas_call(kernel, out_shape=outs, in_specs=[ANY if i in far_in else...  240 us

profile of v2, /device:TPU:193, one launch (start us, length us, event | category | flops | bytes accessed | tf_op | source)
XLA Modules:
  0.0 243.3 jit_solution(14709451606094615062)
XLA Ops:
  0.6 0.0 copy-start
  0.6 1.6 copy-done
  2.2 0.0 copy-start.6
  2.2 0.7 copy-done.6
  2.9 3.3 %pack.1 = (f32[6,256,128]{2,1,0:T(8,128)S(1)}, bf16[512,1152]{1,0:T(8,128)(2,1)S(1)}, bf16[512,1024]{1,0:T(8,128)(2,1)S(1)}) custom-call(bf16[512,2048]{1,0:T(8,128)(2,1)S(1)} %bitcast.6, f32[16,128]{1,0:T(8,128)S(1)} %bitcast.8), custom_call_target="tpu_custom_call" | custom-call | bytes 8388608 | tf_op jit(solution)/shard_map/pack/pallas_call | solution.py:37
  6.2 0.0 copy-start.5
  6.2 54.1 %swap_and_sum.1 = (f32[2,6,256,128]{3,2,1,0:T(8,128)}, bf16[512,1152]{1,0:T(8,128)(2,1)S(1)}, bf16[512,1024]{1,0:T(8,128)(2,1)S(1)}, bf16[512,1024]{1,0:T(8,128)(2,1)S(1)}) custom-call(f32[6,256,128]{2,1,0:T(8,128)S(1)} %get-tuple-element.22.pay, bf16[512,2048]{1,0:T(8,128)(2,1)} %bitcast.3, bf16[512,1152]{1,0:T(8,128)(2,1)S(1)} %get-tuple-element.23.send), custom_call_target="tpu_custom_call" | custom-call | bytes 8388608 | tf_op jit(solution)/shard_map/swap_and_sum/pallas_call | solution.py:37
  60.3 0.0 copy-start.3
  60.3 0.9 cross_overlap.1.pay
  61.3 0.0 copy-done.5
  61.3 67.1 %first_factor.1 = (f32[8,256,128]{2,1,0:T(8,128)S(1)}, f32[512,512]{1,0:T(8,128)S(1)}, bf16[512,1024]{1,0:T(8,128)(2,1)S(1)}, bf16[512,1024]{1,0:T(8,128)(2,1)S(1)}) custom-call(f32[2,6,256,128]{3,2,1,0:T(8,128)} %get-tuple-element.24.s, f32[8,256,128]{2,1,0:T(8,128)S(1)} %cross_overlap.1.pay, bf16[512,2048]{1,0:T(8,128)(2,1)} %bitcast.4), custom_call_target="tpu_custom_call" | custom-call | bytes 8388608 | tf_op jit(solution)/shard_map/first_factor/pallas_call | solution.py:37
  128.4 0.0 copy-done.3
  128.4 16.1 %hamiltonian.1 = (f32[6,256,128]{2,1,0:T(8,128)S(1)}, f32[8,256,128]{2,1,0:T(8,128)S(1)}) custom-call(bf16[512,2048]{1,0:T(8,128)(2,1)} %bitcast.5, bf16[512,1024]{1,0:T(8,128)(2,1)S(1)} %get-tuple-element.29.xlo, bf16[512,1024]{1,0:T(8,128)(2,1)S(1)} %get-tuple-element.30.xhi, bf16[512,1024]{1,0:T(8,128)(2,1)S(1)} %get-tuple-element.31.ylo, ...), custom_call_target="tpu_custom_call" | custom-call | bytes 8388608 | tf_op jit(solution)/shard_map/hamiltonian/pallas_call | solution.py:37
  144.5 0.0 copy-start.2
  144.5 83.5 %second_factor.1 = (f32[512,1024]{1,0:T(8,128)}, f32[2,6,256,128]{3,2,1,0:T(8,128)}, f32[8,256,128]{2,1,0:T(8,128)S(1)}, bf16[512,1024]{1,0:T(8,128)(2,1)S(1)}) custom-call(f32[2,6,256,128]{3,2,1,0:T(8,128)} %get-tuple-element.24.s, f32[8,256,128]{2,1,0:T(8,128)S(1)} %get-tuple-element.27.x, f32[512,512]{1,0:T(8,128)S(1)} %get-tuple-element.28.w0, ...), custom_call_target="tpu_custom_call" | custom-call | bytes 8388608 | tf_op jit(solution)/shard_map/second_factor/pallas_call | solution.py:37
  228.0 0.0 copy-done.2
  228.0 0.0 copy-start.1
  228.1 0.0 copy-start.4
  228.1 9.9 %subspace_matrix.1 = (f32[1024,1024]{1,0:T(8,128)}, bf16[512,512]{1,0:T(8,128)(2,1)S(1)}, bf16[512,512]{1,0:T(8,128)(2,1)S(1)}) custom-call(f32[2,6,256,128]{3,2,1,0:T(8,128)S(1)} %copy-done.2, f32[2,6,256,128]{3,2,1,0:T(8,128)} %get-tuple-element.35.hown, f32[8,256,128]{2,1,0:T(8,128)S(1)} %get-tuple-element.36.cross, f32[512,512]{1,0:T(8,128)S(1)} %get-tuple-element.28.w0, ...), custom_call_target="tpu_custom_call" | custom-call | bytes 8388608 | tf_op jit(solution)/shard_map/subspace_matrix/pallas_call | solution.py:37
  237.9 0.0 copy-done.1
  237.9 0.0 copy-done.4
  237.9 5.2 %rotate.1 = bf16[512,2048]{1,0:T(8,128)(2,1)} custom-call(bf16[512,512]{1,0:T(8,128)(2,1)S(1)} %get-tuple-element.38.rot_other, bf16[512,512]{1,0:T(8,128)(2,1)S(1)} %get-tuple-element.39.rot_own, bf16[512,1152]{1,0:T(8,128)(2,1)S(1)} %copy-done.4, bf16[512,1024]{1,0:T(8,128)(2,1)S(1)} %get-tuple-element.40.rest, bf16[512,2048]{1,0:T(8,128)(2,1)S(1)} %bitcast.7), custom_call_target="tpu_custom_call" | custom-call | bytes 8388608 | tf_op jit(solution)/shard_map/rotate/pallas_call | solution.py:37
Async XLA Ops:
  0.6 1.6 copy-start
  2.2 0.7 copy-start.6
  6.2 55.1 %copy-start.5 = (bf16[512,1024]{1,0:T(8,128)(2,1)}, bf16[512,1024]{1,0:T(8,128)(2,1)S(1)}, u32[]{:S(2)}) copy-start(bf16[512,1024]{1,0:T(8,128)(2,1)S(1)} %get-tuple-element.25.keep) | copy-start | bytes 3145732
  60.3 68.1 %copy-start.3 = (bf16[512,1152]{1,0:T(8,128)(2,1)}, bf16[512,1152]{1,0:T(8,128)(2,1)S(1)}, u32[]{:S(2)}) copy-start(bf16[512,1152]{1,0:T(8,128)(2,1)S(1)} %get-tuple-element.26.recv) | copy-start | bytes 3538948
  144.5 83.5 %copy-start.2 = (f32[2,6,256,128]{3,2,1,0:T(8,128)S(1)}, f32[2,6,256,128]{3,2,1,0:T(8,128)}, u32[]{:S(2)}) copy-start(f32[2,6,256,128]{3,2,1,0:T(8,128)} %get-tuple-element.24.s) | copy-start | bytes 4718596
  228.0 9.9 %copy-start.1 = (bf16[512,1,2048]{2,0,1:T(8,128)(2,1)S(1)}, bf16[512,1,2048]{2,0,1:T(8,128)(2,1)}, u32[]{:S(2)}) copy-start(bf16[512,1,2048]{2,0,1:T(8,128)(2,1)} %param.2) | copy-start | bytes 6291460
  228.1 9.9 %copy-start.4 = (bf16[512,1152]{1,0:T(8,128)(2,1)S(1)}, bf16[512,1152]{1,0:T(8,128)(2,1)}, u32[]{:S(2)}) copy-start(bf16[512,1152]{1,0:T(8,128)(2,1)} %copy-done.3) | copy-start | bytes 3538948

commit v3 on v2

--- a/solution.py
+++ b/solution.py
@@ -57,18 +57,17 @@
 def edge_cells():
     lane = lax.broadcasted_iota(jnp.int32, (128, 128), 1)
     q = lane % 4
-    return lane // 4, jnp.where(q < 2, 64 + q, 124 + q)
-
-
-def pack_kernel(orb, pot, pay, send, keep):
-    band = lax.axis_index("band")
+    return lane // 64, (lane % 64) // 4, jnp.where(q < 2, 64 + q, 124 + q)
+
+
+def pack(band, orb, pot, pay, send, keep, edge_send):
     for t, (r, c) in enumerate(TILES_UP):
         tile = bdot(orb[256 * r : 256 * r + 256, :], orb[256 * c : 256 * c + 256, :], NT)
         pay[2 * t] = tile[:, :128]
         pay[2 * t + 1] = tile[:, 128:]
     pay[0, 128:136, :] = pot[0:8, :] + pot[8:16, :]
     z = lax.broadcasted_iota(jnp.int32, (128, 128), 0)
-    owner, level = edge_cells()
+    side, owner, level = edge_cells()
 
     @pl.loop(0, 4)
     def _(step):
@@ -79,11 +78,16 @@
             for m in range(8):
                 packed = bdot(slab(2 * m), even) + bdot(slab(2 * m + 1), odd)
                 ref[rows, 128 * m : 128 * m + 128] = packed.astype(BF16)
+
+    @pl.loop(0, 2)
+    def _(step):
         edge = jnp.zeros((128, 128), F32)
-        for i in range(16):
-            pick = ((owner == i) & (z == level)).astype(F32).astype(BF16)
-            edge = edge + bdot(slab(i), pick)
-        send[rows, 1024:1152] = edge.astype(BF16)
+        for h in range(2):
+            rows = pl.ds(pl.multiple_of(step * 128, 128) + 256 * h, 128)
+            for i in range(16):
+                pick = ((side == h) & (owner == i) & (z == level)).astype(F32).astype(BF16)
+                edge = edge + bdot(orb[rows, 128 * i : 128 * i + 128], pick)
+        edge_send[pl.ds(pl.multiple_of(step * 128, 128), 128), :] = edge.astype(BF16)
 
 
 class Place:
@@ -180,17 +184,19 @@
 
     def __init__(self, place, both, pay, out, scratch):
         self.place, self.both, self.pay, self.out = place, both, pay, out
+        self.side = pay.shape[1] // 2
+        self.part = self.side // 16
         self.half, self.whole, self.got, self.along = scratch[:4]
         self.s1, self.r1, self.s2, self.r2, self.s3, self.r3, self.s4, self.r4, self.s5, self.r5 = scratch[4:14]
 
     @staticmethod
-    def scratch(n):
+    def scratch(n, height=256, wire=F32):
         dma = pltpu.SemaphoreType.DMA
         return [
-            pltpu.VMEM((n, 128, 128), F32),
-            pltpu.VMEM((n, 128, 128), F32),
-            pltpu.VMEM((16, n, 8, 128), F32),
-            pltpu.VMEM((8, n, 8, 128), F32),
+            pltpu.VMEM((n, height // 2, 128), wire),
+            pltpu.VMEM((n, height // 2, 128), wire),
+            pltpu.VMEM((16, n, height // 32, 128), wire),
+            pltpu.VMEM((8, n, height // 32, 128), wire),
             dma((1,)),
             dma((1,)),
             dma((16,)),
@@ -203,22 +209,24 @@
             dma((16,)),
         ]
 
+    def rows(self, start, count=1):
+        return pl.ds(pl.multiple_of(start * self.part, self.part), count * self.part)
+
     def first(self):
         p = self.place
-        theirs = pl.ds(pl.multiple_of((1 - p.core) * 128, 128), 128)
+        theirs = self.rows((1 - p.core) * 16, 16)
         return remote(self.pay.at[:, theirs, :], self.half, self.s1.at[0], self.r1.at[0], p.partner)
 
     def second(self, k):
         device, there = self.place.xy_peer(k)
-        rows = pl.ds(pl.multiple_of(there * 8, 8), 8)
-        return remote(self.whole.at[:, rows, :], self.got.at[k], self.s2.at[k], self.r2.at[k], device)
+        return remote(self.whole.at[:, self.rows(there), :], self.got.at[k], self.s2.at[k], self.r2.at[k], device)
 
     def third(self, k):
         p = self.place
         return remote(self.along.at[p.zz], self.along.at[p.zz], self.s3.at[k], self.r3.at[k], p.z_peer(k))
 
     def spot(self, row):
-        rows = pl.ds(pl.multiple_of(self.place.core * 128 + row * 8, 8), 8)
+        rows = self.rows(self.place.core * 16 + row)
         return self.out.at[:, :, rows, :] if self.both else self.out.at[:, rows, :]
 
     def fourth(self, k, row):
@@ -234,8 +242,9 @@
 
     def part2(self):
         self.first().wait()
-        mine = pl.ds(pl.multiple_of(self.place.core * 128, 128), 128)
-        self.whole[...] = self.pay[:, mine, :] + self.half[...]
+        mine = self.rows(self.place.core * 16, 16)
+        both = self.pay[:, mine, :].astype(F32) + self.half[...].astype(F32)
+        self.whole[...] = both.astype(self.whole.dtype)
         for k in range(1, 16):
             self.second(k).start()
 
@@ -243,10 +252,10 @@
         p = self.place
         for k in range(1, 16):
             self.second(k).wait()
-        total = self.whole[:, pl.ds(pl.multiple_of(p.here * 8, 8), 8), :]
+        total = self.whole[:, self.rows(p.here), :].astype(F32)
         for k in range(1, 16):
-            total = total + self.got[k]
-        self.along[p.zz] = total
+            total = total + self.got[k].astype(F32)
+        self.along[p.zz] = total.astype(self.along.dtype)
         for k in range(1, 8):
             self.third(k).start()
 
@@ -254,10 +263,10 @@
         p = self.place
         for k in range(1, 8):
             self.third(k).wait()
-        along = self.along
+        along = [self.along[i].astype(F32) for i in range(8)]
         lower = along[0] + along[1] + along[2] + along[3]
         upper = along[4] + along[5] + along[6] + along[7]
-        rows = pl.ds(pl.multiple_of(p.core * 128 + p.here * 8, 8), 8)
+        rows = self.rows(p.core * 16 + p.here)
         if self.both:
             self.out[0, :, rows, :] = lower
             self.out[1, :, rows, :] = upper
@@ -310,9 +319,15 @@
             x = jnp.where(sub == s, done[s], x)
         rows[p] = x
         if p < 15:
-            right = jnp.where(lane >= k + 8, x, 0.0)
+            ahead = jnp.where(inside, 0.0, rows[p + 1])
+            pick = lane == k + 8 + sub
+            for r in range(8):
+                ahead = ahead - jnp.sum(jnp.where(pick, done[r], 0.0), axis=1, keepdims=True) * done[r]
+            rows[p + 1] = ahead
+        if p < 14:
+            right = jnp.where(lane >= k + 16, x, 0.0)
             update = fdot(right, x, TN)
-            for q in range(p + 1, 16):
+            for q in range(p + 2, 16):
                 rows[q] = jnp.where(inside, 0.0, rows[q]) - update[8 * q : 8 * q + 8]
     whole = jnp.concatenate(rows, axis=0)
     rr = lax.broadcasted_iota(jnp.int32, (128, 128), 0)
@@ -349,105 +364,111 @@
             c[256 * r : 256 * r + 256, lo : lo + 128] = slabs(2 * t + h)
 
 
-def swap_kernel(pay, orb, send, s_sum, recv, xlo, xhi, *scratch):
+def first_factor_kernel(
+    orb, orb_far, pot, s_sum, w, h_pay, half, edge, keep, recv, edge_recv, *scratch
+):
     place = Place()
-    total = Sum(place, True, pay, s_sum, scratch[:14])
+    s_pay = scratch[23]
+    total = Sum(place, True, s_pay, s_sum, scratch[:14])
     sems = scratch[14:16]
-    rows = lambda n, i: pl.ds((HALF // n) * i, HALF // n)
-    swap = Bulk([(send.at[rows(8, i), :], recv.at[rows(8, i), :]) for i in range(8)], place.opposite, sems, 0)
-    up = Bulk(
-        [(orb.at[rows(4, i), pl.ds(1024, 1024)], xlo.at[rows(4, i), :]) for i in range(4)], place.next_x, sems, 8
+    xlo, xhi, ylo, yhi, hpsi, send, edge_send = scratch[16:23]
+    rows = lambda i: pl.ds(64 * i, 64)
+    pieces = [(edge_send, edge_recv)] + [(send.at[rows(i), :], recv.at[rows(i), :]) for i in range(8)]
+    swap = Bulk(pieces, place.opposite, sems, 0)
+    quarters = [pl.ds(128 * i, 128) for i in range(4)]
+    x_up = Bulk(
+        [(orb_far.at[q, pl.ds(1024, 1024)], xlo.at[q, :]) for q in quarters], place.next_x, sems, 9
     )
-    down = Bulk(
-        [(orb.at[rows(4, i), pl.ds(0, 1024)], xhi.at[rows(4, i), :]) for i in range(4)], place.last_x, sems, 12
-    )
-    place.greet(False)
-    total.part1()
-    swap.start(2)
-    total.part2()
-    up.start()
-    down.start()
-    total.part3()
-    swap.start()
-    total.part4()
-    total.part5()
-    total.end()
-    up.wait()
-    down.wait()
-    swap.wait()
-
-
-def first_factor_kernel(s, pay, orb, x_sum, w, ylo, yhi, *scratch):
-    place = Place()
-    total = Sum(place, False, pay, x_sum, scratch[:14])
-    sems = scratch[14:16]
-    up = Bulk(
-        [(orb.at[:, pl.ds(512 * a + 256, 256)], ylo.at[:, pl.ds(256 * a, 256)]) for a in range(4)],
+    x_down = Bulk([(orb_far.at[q, pl.ds(0, 1024)], xhi.at[q, :]) for q in quarters], place.last_x, sems, 13)
+    y_up = Bulk(
+        [(orb_far.at[:, pl.ds(512 * a + 256, 256)], ylo.at[:, pl.ds(256 * a, 256)]) for a in range(4)],
         place.next_y,
         sems,
-        0,
+        17,
     )
-    down = Bulk(
-        [(orb.at[:, pl.ds(512 * a, 256)], yhi.at[:, pl.ds(256 * a, 256)]) for a in range(4)], place.last_y, sems, 4
+    y_down = Bulk(
+        [(orb_far.at[:, pl.ds(512 * a, 256)], yhi.at[:, pl.ds(256 * a, 256)]) for a in range(4)],
+        place.last_y,
+        sems,
+        21,
     )
     place.greet(True)
+    y_up.start()
+    pack(place.band, orb, pot, s_pay, send, keep, edge_send)
     total.part1()
+    total.part2()
+    x_up.start()
+    x_down.start()
+    total.part3()
+    y_down.start()
+    edge_differences(place.band, orb, edge)
+    total.part4()
+    swap.start()
+    x_up.wait()
+    x_down.wait()
+    total.part5()
+    y_up.wait()
+    y_down.wait()
+    hamiltonian(place.band, orb, xlo, xhi, ylo, yhi, pot, hpsi, half)
+    for t, (r, c) in enumerate(TILES_LOW):
+        tile = bdot(hpsi[256 * r : 256 * r + 256, :], orb[256 * c : 256 * c + 256, :], NT)
+        store_tall(h_pay, t, tile)
+    total.end()
     w[256:512, 0:256] = jnp.zeros((256, 256), F32)
-    spread(w, lambda i: s[0, i], TILES_UP, 0)
-    total.part2()
-    eliminate_step(w, 0, 0)
-    total.part3()
-    up.start()
-    down.start()
-    eliminate_step(w, 0, 1)
-    total.part4()
-    eliminate_step(w, 0, 2)
-    total.part5()
-    eliminate_step(w, 0, 3)
+    spread(w, lambda i: s_sum[0, i], TILES_UP, 0)
+    for j in range(4):
+        eliminate_step(w, 0, j)
     clear_right(w, 0)
-    total.end()
-    up.wait()
-    down.wait()
-
-
-def second_factor_kernel(s, x, w0, hown, hcross, keep, c, hown_sum, hcross_sum, rest, *scratch):
+    swap.wait()
+
+
+def second_factor_kernel(
+    s, h_pay, half, edge, keep, keep_far, recv, edge_recv, w0, c, own_sum, cross_sum, rest, *scratch
+):
     place = Place()
-    own = Sum(place, True, hown, hown_sum, scratch[:14])
-    cross = Sum(place, False, hcross, hcross_sum, scratch[14:28])
-    sems = scratch[28:30]
-    cross_s = scratch[30]
+    x_pay, x_sum, cross_pay, cross_s = scratch[42:46]
+    over = Sum(place, False, x_pay, x_sum, scratch[:14])
+    own = Sum(place, True, h_pay, own_sum, scratch[14:28])
+    cross = Sum(place, False, cross_pay, cross_sum, scratch[28:42])
+    sems = scratch[46:48]
     rows = lambda i: pl.ds(64 * i, 64)
-    tail = Bulk(
-        [(keep.at[rows(i), :], rest.at[rows(i), :]) for i in range(8)],
-        place.opposite,
-        sems,
-        0,
-        place.band == 0,
-        place.band == 1,
-    )
+    pieces = [(keep_far.at[rows(i), :], rest.at[rows(i), :]) for i in range(8)]
+    tail = Bulk(pieces, place.opposite, sems, 0, place.band == 0, place.band == 1)
     place.greet(False)
     own.part1()
+    tail.start(2)
+    cross_products(place.band, keep, recv, x_pay)
+    over.part1()
+    cross_products(place.band, half, recv, cross_pay, edge, edge_recv)
+    over.part2()
     cross.part1()
+    own.part2()
+    over.part3()
+    tail.start(2)
+    over.part4()
+    cross.part2()
+    own.part3()
+    tail.start(2)
+    over.part5()
+    own.part4()
+    over.end()
     for t, (r, col) in enumerate(TILES_ALL):
         for h in range(2):
             lo = 256 * col + 128 * h
-            cross_s[256 * r : 256 * r + 256, lo : lo + 128] = x[2 * t + h]
-    low = fdot(cross_s[...], w0[...], NT)
+            cross_s[256 * r : 256 * r + 256, lo : lo + 128] = x_sum[2 * t + h]
+    first = split(w0[...])
+    low = split(dot3(split(cross_s[...]), first, NT))
     c[256:512, 512:768] = jnp.zeros((256, 256), F32)
     spread(c, lambda i: s[1, i], TILES_UP, 512)
-    c[:, 512:1024] = c[:, 512:1024] - fdot(low, low, NT)
-    c[:, 0:512] = -fdot(low, w0[...])
-    own.part2()
-    cross.part2()
-    eliminate_step(c, 512, 0)
-    own.part3()
+    c[:, 512:1024] = c[:, 512:1024] - dot3(low, low, NT)
+    c[:, 0:512] = -dot3(low, first)
     cross.part3()
     tail.start()
+    eliminate_step(c, 512, 0)
+    own.part5()
+    cross.part4()
     eliminate_step(c, 512, 1)
-    own.part4()
-    cross.part4()
     eliminate_step(c, 512, 2)
-    own.part5()
     cross.part5()
     eliminate_step(c, 512, 3)
     clear_right(c, 512)
@@ -465,8 +486,17 @@
     return bdot(a[0], b[0], dims) + (bdot(a[0], b[1], dims) + bdot(a[1], b[0], dims))
 
 
-def last_kernel(s, hown, cross, w0, c, h_sub, rot_other, rot_own, wh, wl, mh, ml):
+def last_kernel(
+    s, hown, cross, w0, c, recv_far, rest_far, own_far, h_sub, rotated, rot_other, rot_own, wh, wl, mh, ml, *scratch
+):
     band = lax.axis_index("band")
+    recv, rest, own, out, sems = scratch
+    loads = [
+        pltpu.make_async_copy(far, near, sems.at[i])
+        for i, (far, near) in enumerate(((recv_far, recv), (rest_far, rest), (own_far, own)))
+    ]
+    for load in loads:
+        load.start()
 
     @pl.when(band == 0)
     def _():
@@ -477,6 +507,12 @@
     def _():
         rot_own[...] = c[:, 512:1024].astype(BF16)
         rot_other[...] = c[:, 0:512].astype(BF16)
+
+    for load in loads:
+        load.wait()
+    rotate(band, rot_other, rot_own, recv, rest, own, out)
+    store = pltpu.make_async_copy(out, rotated, sems.at[3])
+    store.start()
 
     for r in range(4):
         source = w0 if r < 2 else c
@@ -490,18 +526,18 @@
     cc = lax.broadcasted_iota(jnp.int32, (256, 256), 1)
     weight = jnp.where(cc < rr, 1.0, jnp.where(cc == rr, 0.5, 0.0)).astype(F32)
 
-    def pair(slabs, t):
-        return jnp.concatenate([slabs(2 * t), slabs(2 * t + 1)], axis=1)
+    def wide(tall):
+        return jnp.concatenate([tall[0:256, :], tall[256:512, :]], axis=1)
 
     half = {}
     for b in range(2):
         for t, (r, col) in enumerate(TILES_LOW):
-            tile = pair(lambda i: hown[b, i], t)
+            tile = wide(hown[b, t])
             if r == col:
                 tile = tile * weight
             half[2 * b + r, 2 * b + col] = split(tile)
     for t, (r, col) in enumerate(TILES_ALL):
-        half[2 + r, col] = split(pair(lambda i: cross[i], t))
+        half[2 + r, col] = split(wide(cross[t]))
 
     def block(high, lowpart, r, col):
         rows, cols = slice(256 * r, 256 * r + 256), slice(256 * col, 256 * col + 256)
@@ -536,6 +572,7 @@
                 tile = tile + product(col, r).T
                 h_sub[256 * r : 256 * r + 256, 256 * col : 256 * col + 256] = tile
                 h_sub[256 * col : 256 * col + 256, 256 * r : 256 * r + 256] = tile.T
+    store.wait()
 
 
 def circle_weights():
@@ -550,18 +587,31 @@
     return jnp.where(near, 16.0, jnp.where(far, -1.0, 0.0))
 
 
-def ham_kernel(orb, xlo, xhi, ylo, yhi, pot, recv, pay, cross, hpsi, half, edge):
-    band = lax.axis_index("band")
+def edge_differences(band, orb, edge):
+    row, _, _ = circle_weights()
+    _, owner, level = edge_cells()
+    weights = jnp.where(row < 64, step_weights((row - level + 128) % 128), 0.0)
+
+    @pl.loop(0, 4)
+    def _(step):
+        rows = pl.ds(pl.multiple_of(step * 128, 128), 128)
+        total = jnp.zeros((128, 128), F32)
+        for i in range(16):
+            total = total + bdot(orb[rows, 128 * i : 128 * i + 128], jnp.where(owner == i, weights, 0.0).astype(BF16))
+        edge[rows, :] = jnp.where(band == 1, total * (-0.5 / 12.0), 0.0).astype(BF16)
+
+
+def hamiltonian(band, orb, xlo, xhi, ylo, yhi, pot, hpsi, half):
     row, col, weights = circle_weights()
     full = jnp.where(row == col, -90.0, weights)
-    inner = jnp.where((band == 1) | ((row >= 64) & (col >= 64)), full, 0.0)
-    full, inner = full.astype(BF16), inner.astype(BF16)
-    owner, level = edge_cells()
-    even, odd = packers(64 - 64 * band)
-
-    @pl.loop(0, 16)
+    outer = jnp.where((band == 0) & (row < 64) & (col >= 64), weights, 0.0)
+    circles = jnp.concatenate([full, outer], axis=1).astype(BF16)
+    pack = jnp.concatenate(packers(64 - 64 * band), axis=0)
+    n = 32
+
+    @pl.loop(0, HALF // n, unroll=2)
     def _(step):
-        rows = pl.ds(pl.multiple_of(step * 32, 32), 32)
+        rows = pl.ds(pl.multiple_of(step * n, n), n)
 
         def slab(ref, i):
             return ref[rows, 128 * i : 128 * i + 128]
@@ -577,48 +627,43 @@
                 return slab(yhi, a * 2 + b - 4)
             return slab(orb, a * 4 + b)
 
-        for pair in range(8):
-            packed = None
-            for i in (2 * pair, 2 * pair + 1):
-                a, b = i // 4, i % 4
-                center = cell(a, b)
-                field = lambda i, j: cell(i, j).astype(F32)
-                near = field(a - 1, b) + field(a + 1, b) + field(a, b - 1) + field(a, b + 1)
-                far = field(a - 2, b) + field(a + 2, b) + field(a, b - 2) + field(a, b + 2)
-                across = 16.0 * near - far
-                base = pot[i : i + 1, :] * center.astype(F32)
-                value = (across + bdot(center, full)) * (-0.5 / 12.0) + base
-                hpsi[rows, 128 * i : 128 * i + 128] = value.astype(BF16)
-                value = (across + bdot(center, inner)) * (-0.5 / 12.0) + base
-                part = bdot(value.astype(BF16), even if i % 2 == 0 else odd)
-                packed = part if packed is None else packed + part
-            half[rows, 128 * pair : 128 * pair + 128] = packed.astype(BF16)
-
-    @pl.loop(0, 4)
-    def _(step):
-        rows = pl.ds(pl.multiple_of(step * 128, 128), 128)
-        total = jnp.zeros((128, 128), F32)
+        cells = jnp.concatenate([cell(i // 4, i % 4) for i in range(16)], axis=0)
+        along = bdot(cells, circles)
+        parts = [[], []]
         for i in range(16):
-            weight = jnp.where((owner == i) & (row < 64), step_weights((row - level + 128) % 128), 0.0)
-            total = total + bdot(orb[rows, 128 * i : 128 * i + 128], weight.astype(BF16))
-        edge[rows, :] = jnp.where(band == 1, total * (-0.5 / 12.0), 0.0).astype(BF16)
-
-    for t, (r, c) in enumerate(TILES_LOW):
-        tile = bdot(hpsi[256 * r : 256 * r + 256, :], orb[256 * c : 256 * c + 256, :], NT)
-        pay[2 * t] = tile[:, :128]
-        pay[2 * t + 1] = tile[:, 128:]
-    cross_products(band, half, recv, cross, edge)
-
-
-def cross_products(band, half, recv, out, edge=None):
+            a, b = i // 4, i % 4
+            field = lambda i, j: cell(i, j).astype(F32)
+            near = (field(a - 1, b) + field(a + 1, b)) + (field(a, b - 1) + field(a, b + 1))
+            far = (field(a - 2, b) + field(a + 2, b)) + (field(a, b - 2) + field(a, b + 2))
+            here = slice(n * i, n * i + n)
+            value = (16.0 * near - far + along[here, :128]) * (-0.5 / 12.0) + pot[i : i + 1, :] * field(a, b)
+            hpsi[rows, 128 * i : 128 * i + 128] = value.astype(BF16)
+            parts[i % 2].append((value + along[here, 128:] * (0.5 / 12.0)).astype(BF16))
+        sides = [jnp.concatenate(part, axis=0) for part in parts]
+        packed = bdot(jnp.concatenate(sides, axis=1), pack)
+        for m in range(8):
+            half[rows, 128 * m : 128 * m + 128] = packed[n * m : n * m + n].astype(BF16)
+
+
+def store_tall(out, t, tile):
+    out[t, 0:256, :] = tile[:, :128].astype(out.dtype)
+    out[t, 256:512, :] = tile[:, 128:].astype(out.dtype)
+
+
+def cross_products(band, half, recv, out, edge=None, edge_recv=None):
     def products(left, right, corner):
         for t, (r, c) in enumerate(TILES_ALL):
             up, across = slice(256 * r, 256 * r + 256), slice(256 * c, 256 * c + 256)
             tile = bdot(left[up, 0:1024], right[across, 0:1024], NT)
             if corner:
-                tile = tile + bdot(edge[up, :], recv[across, 1024:1152], NT)
-            out[2 * t] = tile[:, :128]
-            out[2 * t + 1] = tile[:, 128:]
+                lane = lax.broadcasted_iota(jnp.int32, (256, 128), 1)
+                corner_part = jnp.where(lane // 64 == c, edge[up, :].astype(F32), 0.0).astype(BF16)
+                tile = tile + bdot(corner_part, edge_recv[...], NT)
+            if edge is None:
+                out[2 * t] = tile[:, :128]
+                out[2 * t + 1] = tile[:, 128:]
+            else:
+                store_tall(out, t, tile)
 
     @pl.when(band == 1)
     def _():
@@ -629,13 +674,7 @@
         products(recv, half, False)
 
 
-def cross_kernel(keep, recv, out):
-    cross_products(lax.axis_index("band"), keep, recv, out)
-
-
-def rotate_kernel(rot_other, rot_own, recv, rest, own, out):
-    band = lax.axis_index("band")
-
+def rotate(band, rot_other, rot_own, recv, rest, own, out):
     @pl.when(band == 0)
     def _():
         for i in range(4):
@@ -663,55 +702,50 @@
     slab = lambda n: jax.ShapeDtypeStruct((n, 256, 128), F32)
     square = lambda n, t: jax.ShapeDtypeStruct((n, n), t)
     wide = lambda n: jax.ShapeDtypeStruct((HALF, n), BF16)
+    tall = lambda n, t, *lead: jax.ShapeDtypeStruct(lead + (n, 512, 128), t)
     two = lambda n: jax.ShapeDtypeStruct((2, n, 256, 128), F32)
     dma = pltpu.SemaphoreType.DMA
-    s_pay, send, keep = call(pack_kernel, [slab(6), wide(1152), wide(1024)], (orb, pot), "pack")
-    s_sum, recv, xlo, xhi = call(
-        swap_kernel,
-        [two(6), wide(1152), wide(1024), wide(1024)],
-        (s_pay, orb, send),
-        "swap_and_sum",
-        scratch=Sum.scratch(6) + [dma((16,)), dma((16,))],
+    corner = jax.ShapeDtypeStruct((256, 128), BF16)
+    s_sum, w0, h_pay, half, edge, keep, recv, edge_recv = call(
+        first_factor_kernel,
+        [two(6), square(512, F32), tall(3, F32), wide(1024), wide(128), wide(1024), wide(1024), corner],
+        (orb, orb, pot),
+        "first_factor",
+        scratch=Sum.scratch(6)
+        + [dma((25,)), dma((25,))]
+        + [pltpu.VMEM((HALF, n), BF16) for n in (1024, 1024, 1024, 1024, CELLS, 1024)]
+        + [pltpu.VMEM((256, 128), BF16), pltpu.VMEM((6, 256, 128), F32)],
         collective=0,
-        far_in=(1, 2),
-        far_out=(1, 2, 3),
-    )
-    (x_pay,) = call(cross_kernel, [slab(8)], (keep, recv), "cross_overlap")
-    x_sum, w0, ylo, yhi = call(
-        first_factor_kernel,
-        [slab(8), square(512, F32), wide(1024), wide(1024)],
-        (s_sum, x_pay, orb),
-        "first_factor",
-        scratch=Sum.scratch(8) + [dma((8,)), dma((8,))],
-        collective=1,
-        far_in=(2,),
-        far_out=(2, 3),
-    )
-    h_pay, hx_pay = call(
-        ham_kernel,
-        [slab(6), slab(8)],
-        (orb, xlo, xhi, ylo, yhi, pot, recv),
-        "hamiltonian",
-        scratch=[pltpu.VMEM((HALF, CELLS), BF16), pltpu.VMEM((HALF, 1024), BF16), pltpu.VMEM((HALF, 128), BF16)],
+        far_in=(1,),
+        far_out=(6, 7),
     )
     c, h_sum, hx_sum, rest = call(
         second_factor_kernel,
-        [jax.ShapeDtypeStruct((HALF, 1024), F32), two(6), slab(8), wide(1024)],
-        (s_sum, x_sum, w0, h_pay, hx_pay, keep),
+        [jax.ShapeDtypeStruct((HALF, 1024), F32), tall(3, F32, 2), tall(4, F32), wide(1024)],
+        (s_sum, h_pay, half, edge, keep, keep, recv, edge_recv, w0),
         "second_factor",
-        scratch=Sum.scratch(6) + Sum.scratch(8) + [dma((8,)), dma((8,)), pltpu.VMEM((512, 512), F32)],
-        collective=2,
+        scratch=Sum.scratch(8)
+        + Sum.scratch(3, 512)
+        + Sum.scratch(4, 512)
+        + [pltpu.VMEM((8, 256, 128), F32)] * 2
+        + [pltpu.VMEM((4, 512, 128), F32), pltpu.VMEM((512, 512), F32)]
+        + [dma((8,)), dma((8,))],
+        collective=1,
         far_in=(5,),
         far_out=(3,),
     )
-    h_sub, rot_other, rot_own = call(
+    h_sub, rotated = call(
         last_kernel,
-        [square(1024, F32), square(512, BF16), square(512, BF16)],
-        (s_sum, h_sum, hx_sum, w0, c),
+        [square(1024, F32), wide(CELLS)],
+        (s_sum, h_sum, hx_sum, w0, c, recv, rest, orb),
         "subspace_matrix",
-        scratch=[pltpu.VMEM((1024, 1024), BF16)] * 4,
+        scratch=[pltpu.VMEM((HALF, HALF), BF16)] * 2
+        + [pltpu.VMEM((1024, 1024), BF16)] * 4
+        + [pltpu.VMEM((HALF, n), BF16) for n in (1024, 1024, CELLS, CELLS)]
+        + [dma((4,))],
+        far_in=(5, 6, 7),
+        far_out=(1,),
     )
-    (rotated,) = call(rotate_kernel, [wide(CELLS)], (rot_other, rot_own, recv, rest, orb), "rotate")
     return rotated.reshape(orbitals.shape), h_sub
 
 

time: 247 us -> 203 us (0.82)
  the two profiles are of different devices: /device:TPU:193 before, /device:TPU:199 now
where the time goes in v3:
time: 203 us; the launch traced here: 200 us
  Pallas kernels  197 us (97%)
    pallas_call x3, Pallas kernels, call(): pl.pallas_call(kernel, out_shape=outs, in_specs=[ANY if i in far_in else...  197 us

profile of v3, /device:TPU:199, one launch (start us, length us, event | category | flops | bytes accessed | tf_op | source)
XLA Modules:
  0.0 200.2 jit_solution(16445959465349686347)
XLA Ops:
  0.6 0.0 copy-start.3
  0.6 0.7 copy-done.3
  1.3 88.4 %first_factor.1 = (f32[2,6,256,128]{3,2,1,0:T(8,128)}, f32[512,512]{1,0:T(8,128)S(1)}, f32[3,512,128]{2,1,0:T(8,128)S(1)}, bf16[512,1024]{1,0:T(8,128)(2,1)S(1)}...) custom-call(bf16[512,2048]{1,0:T(8,128)(2,1)} %bitcast.4, ...), custom_call_target="tpu_custom_call" | custom-call | bytes 8388608 | tf_op jit(solution)/shard_map/first_factor/pallas_call | solution.py:37
  89.7 0.0 copy-start.1
  89.7 1.0 copy-done.1
  90.7 0.0 copy-start
  90.7 0.0 copy-start.2
  90.7 93.5 %second_factor.1 = (f32[512,1024]{1,0:T(8,128)}, f32[2,3,512,128]{3,2,1,0:T(8,128)}, f32[4,512,128]{2,1,0:T(8,128)S(1)}, bf16[512,1024]{1,0:T(8,128)(2,1)S(1)}) custom-call(f32[2,6,256,128]{3,2,1,0:T(8,128)} %get-tuple-element.16.s, f32[3,512,128]{2,1,0:T(8,128)S(1)} %get-tuple-element.17.h_pay, bf16[512,1024]{1,0:T(8,128)(2,1)S(1)} %get-tuple-element.18.half, ...), custom_call_target="tpu_custom_call" | custom-call | bytes 8388608 | tf_op jit(solution)/shard_map/second_factor/pallas_call | solution.py:37
  184.2 0.0 copy-done
  184.2 0.0 copy-done.2
  184.2 15.5 %subspace_matrix.1 = (f32[1024,1024]{1,0:T(8,128)}, bf16[512,2048]{1,0:T(8,128)(2,1)}) custom-call(f32[2,6,256,128]{3,2,1,0:T(8,128)S(1)} %copy-done, f32[2,3,512,128]{3,2,1,0:T(8,128)} %get-tuple-element.24.hown, f32[4,512,128]{2,1,0:T(8,128)S(1)} %get-tuple-element.25.cross, f32[512,512]{1,0:T(8,128)S(1)} %copy-done.2, f32[512,1024]{1,0:T(8,128)} %get-tuple-element.26.c, ...), custom_call_target="tpu_custom_call" | custom-call | bytes 8388608 | tf_op jit(solution)/shard_map/subspace_matrix/pallas_call | solution.py:37
Async XLA Ops:
  0.6 0.7 copy-start.3
  89.7 1.0 copy-start.1
  90.7 93.5 %copy-start = (f32[2,6,256,128]{3,2,1,0:T(8,128)S(1)}, f32[2,6,256,128]{3,2,1,0:T(8,128)}, u32[]{:S(2)}) copy-start(f32[2,6,256,128]{3,2,1,0:T(8,128)} %get-tuple-element.16.s) | copy-start | bytes 4718596
  90.7 93.5 %copy-start.2 = (f32[512,512]{1,0:T(8,128)S(1)}, f32[512,512]{1,0:T(8,128)}, u32[]{:S(2)}) copy-start(f32[512,512]{1,0:T(8,128)} %copy-done.1) | copy-start | bytes 3145732

commit v4 on v3

--- a/solution.py
+++ b/solution.py
@@ -184,8 +184,7 @@
 
     def __init__(self, place, both, pay, out, scratch):
         self.place, self.both, self.pay, self.out = place, both, pay, out
-        self.side = pay.shape[1] // 2
-        self.part = self.side // 16
+        self.part = (out.shape[-2] if pay is None else pay.shape[1]) // 32
         self.half, self.whole, self.got, self.along = scratch[:4]
         self.s1, self.r1, self.s2, self.r2, self.s3, self.r3, self.s4, self.r4, self.s5, self.r5 = scratch[4:14]
 
@@ -248,14 +247,16 @@
         for k in range(1, 16):
             self.second(k).start()
 
-    def part3(self):
-        p = self.place
+    def partial(self):
         for k in range(1, 16):
             self.second(k).wait()
-        total = self.whole[:, self.rows(p.here), :].astype(F32)
+        total = self.whole[:, self.rows(self.place.here), :]
         for k in range(1, 16):
-            total = total + self.got[k].astype(F32)
-        self.along[p.zz] = total.astype(self.along.dtype)
+            total = total + self.got[k]
+        return total
+
+    def part3(self, total=None):
+        self.along[self.place.zz] = self.partial() if total is None else total
         for k in range(1, 8):
             self.third(k).start()
 
@@ -335,7 +336,7 @@
     return jnp.where(cc <= rr, whole, 0.0)
 
 
-def eliminate_step(c, offset, j):
+def eliminate_step(c, offset, j, between=None):
     blocks = c.shape[0] // 128
     rr = lax.broadcasted_iota(jnp.int32, (128, 128), 0)
     cc = lax.broadcasted_iota(jnp.int32, (128, 128), 1)
@@ -343,6 +344,8 @@
     inverse = invert_block(c[rows, cols])
     c[rows, cols] = (rr == cc).astype(F32)
     c[rows, :] = fdot(inverse, c[rows, :])
+    if between is not None:
+        between()
     for i in range(j + 1, blocks):
         below = slice(128 * i, 128 * i + 128)
         across = slice(offset + 128 * i, offset + 128 * i + 128)
@@ -365,32 +368,33 @@
 
 
 def first_factor_kernel(
-    orb, orb_far, pot, s_sum, w, h_pay, half, edge, keep, recv, edge_recv, *scratch
+    orb, orb_far, pot, s_sum, w, h_part, half, edge, keep, recv, edge_recv, *scratch
 ):
     place = Place()
-    s_pay = scratch[23]
+    s_pay, h_pay = scratch[23:25]
+    own = Sum(place, True, h_pay, None, scratch[25:39])
     total = Sum(place, True, s_pay, s_sum, scratch[:14])
     sems = scratch[14:16]
     xlo, xhi, ylo, yhi, hpsi, send, edge_send = scratch[16:23]
-    rows = lambda i: pl.ds(64 * i, 64)
-    pieces = [(edge_send, edge_recv)] + [(send.at[rows(i), :], recv.at[rows(i), :]) for i in range(8)]
+    rows = lambda i: pl.ds(32 * i, 32)
+    pieces = [(edge_send, edge_recv)] + [(send.at[rows(i), :], recv.at[rows(i), :]) for i in range(16)]
     swap = Bulk(pieces, place.opposite, sems, 0)
     quarters = [pl.ds(128 * i, 128) for i in range(4)]
     x_up = Bulk(
-        [(orb_far.at[q, pl.ds(1024, 1024)], xlo.at[q, :]) for q in quarters], place.next_x, sems, 9
+        [(orb_far.at[q, pl.ds(1024, 1024)], xlo.at[q, :]) for q in quarters], place.next_x, sems, 17
     )
-    x_down = Bulk([(orb_far.at[q, pl.ds(0, 1024)], xhi.at[q, :]) for q in quarters], place.last_x, sems, 13)
+    x_down = Bulk([(orb_far.at[q, pl.ds(0, 1024)], xhi.at[q, :]) for q in quarters], place.last_x, sems, 21)
     y_up = Bulk(
         [(orb_far.at[:, pl.ds(512 * a + 256, 256)], ylo.at[:, pl.ds(256 * a, 256)]) for a in range(4)],
         place.next_y,
         sems,
-        17,
+        25,
     )
     y_down = Bulk(
         [(orb_far.at[:, pl.ds(512 * a, 256)], yhi.at[:, pl.ds(256 * a, 256)]) for a in range(4)],
         place.last_y,
         sems,
-        21,
+        29,
     )
     place.greet(True)
     y_up.start()
@@ -403,54 +407,60 @@
     y_down.start()
     edge_differences(place.band, orb, edge)
     total.part4()
-    swap.start()
+    swap.start(6)
+    total.part5()
+    swap.start(3)
     x_up.wait()
     x_down.wait()
-    total.part5()
     y_up.wait()
     y_down.wait()
+    swap.start(3)
     hamiltonian(place.band, orb, xlo, xhi, ylo, yhi, pot, hpsi, half)
+    swap.start()
     for t, (r, c) in enumerate(TILES_LOW):
         tile = bdot(hpsi[256 * r : 256 * r + 256, :], orb[256 * c : 256 * c + 256, :], NT)
         store_tall(h_pay, t, tile)
+    own.part1()
     total.end()
     w[256:512, 0:256] = jnp.zeros((256, 256), F32)
     spread(w, lambda i: s_sum[0, i], TILES_UP, 0)
-    for j in range(4):
+    eliminate_step(w, 0, 0)
+    own.part2()
+    for j in range(1, 4):
         eliminate_step(w, 0, j)
     clear_right(w, 0)
+    h_part[...] = own.partial()
     swap.wait()
 
 
 def second_factor_kernel(
-    s, h_pay, half, edge, keep, keep_far, recv, edge_recv, w0, c, own_sum, cross_sum, rest, *scratch
+    s, h_part, half, edge, keep, keep_far, recv, edge_recv, w0, c, own_sum, cross_sum, rest, *scratch
 ):
     place = Place()
     x_pay, x_sum, cross_pay, cross_s = scratch[42:46]
     over = Sum(place, False, x_pay, x_sum, scratch[:14])
-    own = Sum(place, True, h_pay, own_sum, scratch[14:28])
+    own = Sum(place, True, None, own_sum, scratch[14:28])
     cross = Sum(place, False, cross_pay, cross_sum, scratch[28:42])
     sems = scratch[46:48]
-    rows = lambda i: pl.ds(64 * i, 64)
-    pieces = [(keep_far.at[rows(i), :], rest.at[rows(i), :]) for i in range(8)]
+    rows = lambda i: pl.ds(32 * i, 32)
+    pieces = [(keep_far.at[rows(i), :], rest.at[rows(i), :]) for i in range(16)]
     tail = Bulk(pieces, place.opposite, sems, 0, place.band == 0, place.band == 1)
     place.greet(False)
-    own.part1()
-    tail.start(2)
+    own.part3(h_part[...])
+    tail.start(3)
     cross_products(place.band, keep, recv, x_pay)
     over.part1()
     cross_products(place.band, half, recv, cross_pay, edge, edge_recv)
     over.part2()
     cross.part1()
-    own.part2()
     over.part3()
+    tail.start(1)
+    over.part4()
     tail.start(2)
-    over.part4()
     cross.part2()
-    own.part3()
+    own.part4()
+    over.part5()
     tail.start(2)
-    over.part5()
-    own.part4()
     over.end()
     for t, (r, col) in enumerate(TILES_ALL):
         for h in range(2):
@@ -463,12 +473,16 @@
     c[:, 512:1024] = c[:, 512:1024] - dot3(low, low, NT)
     c[:, 0:512] = -dot3(low, first)
     cross.part3()
+    tail.start(1)
+    own.part5()
+    more = lambda: tail.start(1)
+    eliminate_step(c, 512, 0, more)
+    more()
+    cross.part4()
+    eliminate_step(c, 512, 1, more)
+    more()
+    eliminate_step(c, 512, 2, more)
     tail.start()
-    eliminate_step(c, 512, 0)
-    own.part5()
-    cross.part4()
-    eliminate_step(c, 512, 1)
-    eliminate_step(c, 512, 2)
     cross.part5()
     eliminate_step(c, 512, 3)
     clear_right(c, 512)
@@ -705,16 +719,18 @@
     tall = lambda n, t, *lead: jax.ShapeDtypeStruct(lead + (n, 512, 128), t)
     two = lambda n: jax.ShapeDtypeStruct((2, n, 256, 128), F32)
     dma = pltpu.SemaphoreType.DMA
+    part = jax.ShapeDtypeStruct((3, 16, 128), F32)
     corner = jax.ShapeDtypeStruct((256, 128), BF16)
-    s_sum, w0, h_pay, half, edge, keep, recv, edge_recv = call(
+    s_sum, w0, h_part, half, edge, keep, recv, edge_recv = call(
         first_factor_kernel,
-        [two(6), square(512, F32), tall(3, F32), wide(1024), wide(128), wide(1024), wide(1024), corner],
+        [two(6), square(512, F32), part, wide(1024), wide(128), wide(1024), wide(1024), corner],
         (orb, orb, pot),
         "first_factor",
         scratch=Sum.scratch(6)
-        + [dma((25,)), dma((25,))]
+        + [dma((33,)), dma((33,))]
         + [pltpu.VMEM((HALF, n), BF16) for n in (1024, 1024, 1024, 1024, CELLS, 1024)]
-        + [pltpu.VMEM((256, 128), BF16), pltpu.VMEM((6, 256, 128), F32)],
+        + [pltpu.VMEM((256, 128), BF16), pltpu.VMEM((6, 256, 128), F32), pltpu.VMEM((3, 512, 128), F32)]
+        + Sum.scratch(3, 512),
         collective=0,
         far_in=(1,),
         far_out=(6, 7),
@@ -722,14 +738,14 @@
     c, h_sum, hx_sum, rest = call(
         second_factor_kernel,
         [jax.ShapeDtypeStruct((HALF, 1024), F32), tall(3, F32, 2), tall(4, F32), wide(1024)],
-        (s_sum, h_pay, half, edge, keep, keep, recv, edge_recv, w0),
+        (s_sum, h_part, half, edge, keep, keep, recv, edge_recv, w0),
         "second_factor",
         scratch=Sum.scratch(8)
         + Sum.scratch(3, 512)
         + Sum.scratch(4, 512)
         + [pltpu.VMEM((8, 256, 128), F32)] * 2
         + [pltpu.VMEM((4, 512, 128), F32), pltpu.VMEM((512, 512), F32)]
-        + [dma((8,)), dma((8,))],
+        + [dma((16,)), dma((16,))],
         collective=1,
         far_in=(5,),
         far_out=(3,),

time: 203 us -> 198 us (0.975)
  the two profiles are of different devices: /device:TPU:199 before, /device:TPU:1 now
where the time goes in v4:
time: 198 us; the launch traced here: 195 us
  Pallas kernels  191 us (96%)
  local copies, waits for them, and re-layouts  2.8 us (1%)
    pallas_call x3, Pallas kernels, call(): pl.pallas_call(kernel, out_shape=outs, in_specs=[ANY if i in far_in else...  191 us

profile of v4, /device:TPU:1, one launch (start us, length us, event | category | flops | bytes accessed | tf_op | source)
XLA Modules:
  0.0 195.3 jit_solution(12505717043923503036)
XLA Ops:
  0.6 0.0 copy-start.4
  0.6 0.7 copy-done.4
  1.3 91.5 %first_factor.1 = (f32[2,6,256,128]{3,2,1,0:T(8,128)S(1)}, f32[512,512]{1,0:T(8,128)S(1)}, f32[3,16,128]{2,1,0:T(8,128)S(1)}, bf16[512,1024]{1,0:T(8,128)(2,1)S(...) custom-call(bf16[512,2048]{1,0:T(8,128)(2,1)} %bitcast.4, ...), custom_call_target="tpu_custom_call" | custom-call | bytes 8388608 | tf_op jit(solution)/shard_map/first_factor/pallas_call | solution.py:37
  92.8 0.0 copy-start
  92.8 1.1 copy-done
  94.0 0.0 copy-start.2
  94.0 1.0 copy-done.2
  95.0 0.0 copy-start.1
  95.0 0.0 copy-start.3
  95.0 86.9 %second_factor.1 = (f32[512,1024]{1,0:T(8,128)}, f32[2,3,512,128]{3,2,1,0:T(8,128)}, f32[4,512,128]{2,1,0:T(8,128)S(1)}, bf16[512,1024]{1,0:T(8,128)(2,1)S(1)}) custom-call(f32[2,6,256,128]{3,2,1,0:T(8,128)} %copy-done, f32[3,16,128]{2,1,0:T(8,128)S(1)} %get-tuple-element.17.h_part, bf16[512,1024]{1,0:T(8,128)(2,1)S(1)} %get-tuple-element.18.half, ...), custom_call_target="tpu_custom_call" | custom-call | bytes 8388608 | tf_op jit(solution)/shard_map/second_factor/pallas_call | solution.py:37
  181.8 0.0 copy-done.1
  181.9 0.0 copy-done.3
  181.9 12.9 %subspace_matrix.1 = (f32[1024,1024]{1,0:T(8,128)}, bf16[512,2048]{1,0:T(8,128)(2,1)}) custom-call(f32[2,6,256,128]{3,2,1,0:T(8,128)S(1)} %copy-done.1, f32[2,3,512,128]{3,2,1,0:T(8,128)} %get-tuple-element.24.hown, f32[4,512,128]{2,1,0:T(8,128)S(1)} %get-tuple-element.25.cross, f32[512,512]{1,0:T(8,128)S(1)} %copy-done.3, f32[512,1024]{1,0:T(8,128)} %get-tuple-element.26.c, ...), custom_call_target="tpu_custom_call" | custom-call | bytes 8388608 | tf_op jit(solution)/shard_map/subspace_matrix/pallas_call | solution.py:37
Async XLA Ops:
  0.6 0.7 copy-start.4
  92.8 1.1 copy-start
  94.0 1.0 copy-start.2
  95.0 86.9 %copy-start.1 = (f32[2,6,256,128]{3,2,1,0:T(8,128)S(1)}, f32[2,6,256,128]{3,2,1,0:T(8,128)}, u32[]{:S(2)}) copy-start(f32[2,6,256,128]{3,2,1,0:T(8,128)} %copy-done) | copy-start | bytes 4718596
  95.0 86.9 %copy-start.3 = (f32[512,512]{1,0:T(8,128)S(1)}, f32[512,512]{1,0:T(8,128)}, u32[]{:S(2)}) copy-start(f32[512,512]{1,0:T(8,128)} %copy-done.2) | copy-start | bytes 3145732

commit v5 on v4

--- a/solution.py
+++ b/solution.py
@@ -501,7 +501,7 @@
 
 
 def last_kernel(
-    s, hown, cross, w0, c, recv_far, rest_far, own_far, h_sub, rotated, rot_other, rot_own, wh, wl, mh, ml, *scratch
+    s, hown, cross, w0, c, recv_far, rest_far, own_far, h_sub, rotated, rot_other, rot_own, wh, wl, mh, ml, g, *scratch
 ):
     band = lax.axis_index("band")
     recv, rest, own, out, sems = scratch
@@ -553,39 +553,42 @@
     for t, (r, col) in enumerate(TILES_ALL):
         half[2 + r, col] = split(wide(cross[t]))
 
-    def block(high, lowpart, r, col):
+    def stripe(high, lowpart, k):
+        rows, cols = slice(256 * k, 1024), slice(256 * k, 256 * k + 256)
+        return high[rows, cols], lowpart[rows, cols]
+
+    def square(high, lowpart, r, col):
         rows, cols = slice(256 * r, 256 * r + 256), slice(256 * col, 256 * col + 256)
         return high[rows, cols], lowpart[rows, cols]
 
-    for r in range(4):
-        for col in range(r + 1):
-            total = None
-            for k in range(col, r + 1):
-                part = dot3(block(wh, wl, r, k), half[k, col])
-                total = part if total is None else total + part
-            high, lowpart = split(total)
-            mh[256 * r : 256 * r + 256, 256 * col : 256 * col + 256] = high
-            ml[256 * r : 256 * r + 256, 256 * col : 256 * col + 256] = lowpart
+    for col in range(4):
+        g[256 * col : 1024, :] = dot3(stripe(wh, wl, col), half[col, col])
+        for k in range(col + 1, 4):
+            g[256 * k : 1024, :] = g[256 * k : 1024, :] + dot3(stripe(wh, wl, k), half[k, col])
+        high, lowpart = split(g[256 * col : 1024, :])
+        mh[256 * col : 1024, 256 * col : 256 * col + 256] = high
+        ml[256 * col : 1024, 256 * col : 256 * col + 256] = lowpart
 
     vmean = jnp.sum(s[0, 0, 128:136, :]) / (128 * CELLS)
     shift = jnp.where(rr == cc, vmean, 0.0)
 
-    def product(r, col):
-        total = None
-        for k in range(min(r, col) + 1):
-            part = dot3(block(mh, ml, r, k), block(wh, wl, col, k), NT)
-            total = part if total is None else total + part
-        return total
-
+    for col in range(4):
+        cols = slice(256 * col, 256 * col + 256)
+        h_sub[:, cols] = dot3(stripe(mh, ml, 0), square(wh, wl, col, 0), NT)
+        for k in range(1, col + 1):
+            rows = slice(256 * k, 1024)
+            h_sub[rows, cols] = h_sub[rows, cols] + dot3(stripe(mh, ml, k), square(wh, wl, col, k), NT)
     for r in range(4):
+        up = slice(256 * r, 256 * r + 256)
         for col in range(r + 1):
-            tile = product(r, col)
+            across = slice(256 * col, 256 * col + 256)
             if r == col:
-                h_sub[256 * r : 256 * r + 256, 256 * r : 256 * r + 256] = tile + tile.T - shift
+                tile = h_sub[up, up]
+                h_sub[up, up] = tile + tile.T - shift
             else:
-                tile = tile + product(col, r).T
-                h_sub[256 * r : 256 * r + 256, 256 * col : 256 * col + 256] = tile
-                h_sub[256 * col : 256 * col + 256, 256 * r : 256 * r + 256] = tile.T
+                tile = h_sub[up, across] + h_sub[across, up].T
+                h_sub[up, across] = tile
+                h_sub[across, up] = tile.T
     store.wait()
 
 
@@ -697,14 +700,12 @@
 
     @pl.when(band == 1)
     def _():
-        low_even, low_odd = packers(0)
-        high_even, high_odd = packers(64)
+        low = jnp.concatenate(packers(0), axis=0)
+        high = jnp.concatenate(packers(64), axis=0)
+        unpack = jnp.concatenate([low, high], axis=1)
         for m in range(8):
             cols = slice(128 * m, 128 * m + 128)
-            low, high = recv[:, cols], rest[:, cols]
-            even = (bdot(low, low_even, NT) + bdot(high, high_even, NT)).astype(BF16)
-            odd = (bdot(low, low_odd, NT) + bdot(high, high_odd, NT)).astype(BF16)
-            other = jnp.concatenate([even, odd], axis=1)
+            other = bdot(jnp.concatenate([recv[:, cols], rest[:, cols]], axis=1), unpack, NT).astype(BF16)
             there = slice(256 * m, 256 * m + 256)
             total = bdot(rot_own[...], own[:, there]) + bdot(rot_other[...], other)
             out[:, there] = total.astype(BF16)
@@ -757,6 +758,7 @@
         "subspace_matrix",
         scratch=[pltpu.VMEM((HALF, HALF), BF16)] * 2
         + [pltpu.VMEM((1024, 1024), BF16)] * 4
+        + [pltpu.VMEM((1024, 256), F32)]
         + [pltpu.VMEM((HALF, n), BF16) for n in (1024, 1024, CELLS, CELLS)]
         + [dma((4,))],
         far_in=(5, 6, 7),

time: 198 us -> 198 us (level)
  no operation moved by 1% of the time
where the time goes in v5:
time: 198 us; the launch traced here: 195 us
  Pallas kernels  191 us (96%)
  local copies, waits for them, and re-layouts  2.8 us (1%)
    pallas_call x3, Pallas kernels, call(): pl.pallas_call(kernel, out_shape=outs, in_specs=[ANY if i in far_in else...  191 us

profile of v5, /device:TPU:1, one launch (start us, length us, event | category | flops | bytes accessed | tf_op | source)
XLA Modules:
  0.0 194.9 jit_solution(3371172572030426726)
XLA Ops:
  0.6 0.0 copy-start.4
  0.6 0.7 copy-done.4
  1.3 91.5 %first_factor.1 = (f32[2,6,256,128]{3,2,1,0:T(8,128)S(1)}, f32[512,512]{1,0:T(8,128)S(1)}, f32[3,16,128]{2,1,0:T(8,128)S(1)}, bf16[512,1024]{1,0:T(8,128)(2,1)S(...) custom-call(bf16[512,2048]{1,0:T(8,128)(2,1)} %bitcast.4, ...), custom_call_target="tpu_custom_call" | custom-call | bytes 8388608 | tf_op jit(solution)/shard_map/first_factor/pallas_call | solution.py:37
  92.8 0.0 copy-start
  92.8 1.1 copy-done
  94.0 0.0 copy-start.2
  94.0 1.0 copy-done.2
  94.9 0.0 copy-start.1
  94.9 0.0 copy-start.3
  94.9 86.9 %second_factor.1 = (f32[512,1024]{1,0:T(8,128)}, f32[2,3,512,128]{3,2,1,0:T(8,128)}, f32[4,512,128]{2,1,0:T(8,128)S(1)}, bf16[512,1024]{1,0:T(8,128)(2,1)S(1)}) custom-call(f32[2,6,256,128]{3,2,1,0:T(8,128)} %copy-done, f32[3,16,128]{2,1,0:T(8,128)S(1)} %get-tuple-element.17.h_part, bf16[512,1024]{1,0:T(8,128)(2,1)S(1)} %get-tuple-element.18.half, ...), custom_call_target="tpu_custom_call" | custom-call | bytes 8388608 | tf_op jit(solution)/shard_map/second_factor/pallas_call | solution.py:37
  181.8 0.0 copy-done.1
  181.8 0.0 copy-done.3
  181.8 12.8 %subspace_matrix.1 = (f32[1024,1024]{1,0:T(8,128)}, bf16[512,2048]{1,0:T(8,128)(2,1)}) custom-call(f32[2,6,256,128]{3,2,1,0:T(8,128)S(1)} %copy-done.1, f32[2,3,512,128]{3,2,1,0:T(8,128)} %get-tuple-element.24.hown, f32[4,512,128]{2,1,0:T(8,128)S(1)} %get-tuple-element.25.cross, f32[512,512]{1,0:T(8,128)S(1)} %copy-done.3, f32[512,1024]{1,0:T(8,128)} %get-tuple-element.26.c, ...), custom_call_target="tpu_custom_call" | custom-call | bytes 8388608 | tf_op jit(solution)/shard_map/subspace_matrix/pallas_call | solution.py:37
Async XLA Ops:
  0.6 0.7 copy-start.4
  92.8 1.1 copy-start
  94.0 1.0 copy-start.2
  94.9 86.9 %copy-start.1 = (f32[2,6,256,128]{3,2,1,0:T(8,128)S(1)}, f32[2,6,256,128]{3,2,1,0:T(8,128)}, u32[]{:S(2)}) copy-start(f32[2,6,256,128]{3,2,1,0:T(8,128)} %copy-done) | copy-start | bytes 4718596
  94.9 86.9 %copy-start.3 = (f32[512,512]{1,0:T(8,128)S(1)}, f32[512,512]{1,0:T(8,128)}, u32[]{:S(2)}) copy-start(f32[512,512]{1,0:T(8,128)} %copy-done.2) | copy-start | bytes 3145732
